TPU v7x, 32 devices: a whole 2x2x4 slice. The times are simulated.
32 devices in a mesh: dp: 16 (over z, x, core), mp: 2 (over y).
Axes of the slice: x: 2, y: 2, z: 4, core: 2. Of those that a mesh axis runs over, the one named last changes fastest.
Arguments:
- tokens: bfloat16 [16, 1089, 768], P('dp'), may hold values from -6 to 6
- cotangent: bfloat16 [16, 1089, 768], P('dp'), may hold values from -6 to 6
- long_flag: int32 [16], P('dp'), may hold values from 0 to 1, as said below
- token_mask: int32 [16, 1089], P('dp'), may hold values from 0 to 1, as said below
- bucket_line: int32 [16, 1089, 1089], P('dp'), may hold values from 0 to 31
- bucket_across: int32 [16, 1089, 1089], P('dp'), may hold values from 0 to 63
- bucket_down: int32 [16, 1089, 1089], P('dp'), may hold values from 0 to 63
- project_weight: bfloat16 [3, 768, 768], P(None, None, 'mp'), may hold values from -0.21875 to 0.21875
- project_bias: bfloat16 [2, 768], P(None, 'mp'), may hold values from -4 to 4
- table_line: bfloat16 [32, 12], P(None, 'mp'), may hold values from -6 to 6
- table_across: bfloat16 [64, 12], P(None, 'mp'), may hold values from -6 to 6
- table_down: bfloat16 [64, 12], P(None, 'mp'), may hold values from -6 to 6
- output_weight: bfloat16 [768, 768], P('mp'), may hold values from -1.75 to 1.75
- output_bias: bfloat16 [768], replicated, may hold values from -4 to 4
- first_gain: float32 [768], replicated, may hold values from 0.5 to 1.5
- first_shift: float32 [768], replicated, may hold values from -4 to 4
- expand_weight: bfloat16 [768, 3072], P(None, 'mp'), may hold values from -0.21875 to 0.21875
- expand_bias: bfloat16 [3072], P('mp'), may hold values from -4 to 4
- reduce_weight: bfloat16 [3072, 768], P('mp'), may hold values from -0.109375 to 0.109375
- reduce_bias: bfloat16 [768], replicated, may hold values from -4 to 4
- second_gain: float32 [768], replicated, may hold values from 0.5 to 1.5
- second_shift: float32 [768], replicated, may hold values from -4 to 4
Outputs:
- layer_out: bfloat16 [16, 1089, 768], P('dp')
- input_grad: float32 [16, 1089, 768], P('dp', None, 'mp')
- project_weight_grad: float32 [3, 768, 768], P(None, None, 'mp')
- project_bias_grad: float32 [2, 768], P(None, 'mp')
- table_line_grad: float32 [32, 12], P(None, 'mp')
- table_across_grad: float32 [64, 12], P(None, 'mp')
- table_down_grad: float32 [64, 12], P(None, 'mp')
- output_weight_grad: float32 [768, 768], P('mp')
- output_bias_grad: float32 [768], replicated
- first_gain_grad: float32 [768], P('mp')
- first_shift_grad: float32 [768], P('mp')
- expand_weight_grad: float32 [768, 3072], P(None, 'mp')
- expand_bias_grad: float32 [3072], P('mp')
- reduce_weight_grad: float32 [3072, 768], P('mp')
- reduce_bias_grad: float32 [768], replicated
- second_gain_grad: float32 [768], replicated
- second_shift_grad: float32 [768], replicated
Inputs may be any that keep to these rules, and one draw needn't show every extreme that they name: `long_flag`: 1 marks an item of the long bucket (1089 rows), 0 one of the short bucket (709 rows); both kinds occur. `token_mask`: 1 on an item's first rows and 0 after them; an item of the long bucket has more than 709 ones; an item of the short bucket has 532 ones or more, and its ones may run past row 709; some item of each bucket has ones on all 1089 rows.
All inputs are finite; a program needn't handle non-finite values.
Results may differ from a plain program's by a relative error of at most 0.014.
Values may be sent and summed in bfloat16 or wider, within the bound.
A program may use at most 256 MiB of HBM per device.

v0:
```python
from functools import partial

import jax
import jax.numpy as jnp
from jax import lax
from jax.experimental import pallas as pl
from jax.experimental.pallas import tpu as pltpu
from jax.sharding import PartitionSpec as P

LONG = 1089
SHORT = 709
HEAD = 64
LANES = 128
STRIP = 16
BLOCK_ROWS = 224
FEED_PIECE = 768
FEED_STRIP = 112
TABLE_STRIPS = 2
ATTEND_STRIPS = 7

large_negative = -1000000000.0
norm_epsilon = 1e-05
vmem_limit = 56 * 2**20
FINISH_VMEM = 62 * 2**20
bf16 = jnp.bfloat16
f32 = jnp.float32


def round_up(value, step):
    return (value + step - 1) // step * step


def whole_spec(array):
    zeros = (0,) * array.ndim
    return pl.BlockSpec(array.shape, lambda i: zeros)


def dot_f32(left, right):
    return jnp.dot(left, right, preferred_element_type=f32)


def gather_lanes(values, index):
    dims = lax.GatherDimensionNumbers(
        offset_dims=(),
        collapsed_slice_dims=(1,),
        start_index_map=(1,),
        operand_batching_dims=(0,),
        start_indices_batching_dims=(0,),
    )
    return lax.gather(
        values,
        index[..., None],
        dims,
        slice_sizes=(1, 1),
        mode=lax.GatherScatterMode.PROMISE_IN_BOUNDS,
    )


def quarter_rows(ref, quarter):
    count = ref.shape[0] // 4
    return pl.ds(pl.multiple_of(quarter * count, STRIP), count)


def prepare_kernel(
    token_ref,
    weight_ref,
    bias_ref,
    line_ref,
    across_ref,
    down_ref,
    flag_ref,
    mask_ref,
    expand_ref,
    query_ref,
    key_ref,
    key_turned_ref,
    value_ref,
    value_turned_ref,
    token_out_ref,
    plane_ref,
    down_out_ref,
    valid_ref,
    quarter_ref,
    row_ref,
    send_sem,
    recv_sem,
    *,
    length,
    line_count,
):
    step = pl.program_id(0)
    across_mp = {"mp": 1 - lax.axis_index("mp")}
    fetch = pltpu.make_async_remote_copy(
        src_ref=expand_ref.at[quarter_rows(expand_ref, lax.axis_index("dp") % 4), :],
        dst_ref=quarter_ref,
        send_sem=send_sem,
        recv_sem=recv_sem,
        device_id=across_mp,
        device_id_type=pl.DeviceIdType.MESH,
    )

    @pl.when(step == 0)
    def _():
        barrier = pltpu.get_barrier_semaphore()
        pl.semaphore_signal(
            barrier, inc=1, device_id=across_mp, device_id_type=pl.DeviceIdType.MESH
        )
        pl.semaphore_wait(barrier, 1)
        fetch.start()
        limit = jnp.where(flag_ref[0] > 0, LONG, SHORT)
        position = lax.broadcasted_iota(jnp.int32, (1, length), 1)
        row_ref[...] = jnp.zeros_like(row_ref)
        row_ref[0:1, :length] = jnp.where((mask_ref[...] > 0) & (position < limit), 1.0, 0.0)

    pl.when(step == pl.num_programs(0) - 1)(fetch.wait)
    rows = token_ref.shape[0]
    keys = plane_ref.shape[1]
    place = pl.program_id(0) * rows + lax.broadcasted_iota(jnp.int32, token_ref.shape, 0)
    token = jnp.where(place < length, token_ref[...].astype(f32), 0.0).astype(bf16)
    token_out_ref[...] = token
    bias = bias_ref[...].astype(f32)
    query = (dot_f32(token, weight_ref[0]) + bias[0:1, :]).astype(bf16)
    query_ref[...] = (query.astype(f32) * 0.125).astype(bf16)
    key = dot_f32(token, weight_ref[1])
    value = dot_f32(token, weight_ref[2]) + bias[1:2, :]
    away = jnp.where(row_ref[0:1, :] > 0, 0, line_count)
    inside = pl.program_id(0) * rows + lax.broadcasted_iota(jnp.int32, (rows, length), 0) < length
    line = line_ref[...].reshape(rows, length)
    across = across_ref[...].reshape(rows, length)
    down = down_ref[...].reshape(rows, length)
    plane = jnp.where(inside, line | (across << 8), 0) | away[:, :length]
    plane_ref[:, :length] = plane.astype(jnp.int16)
    plane_ref[:, length:] = jnp.full((rows, keys - length), line_count, jnp.int16)
    here = pl.ds(pl.multiple_of(step * rows, LANES), rows)
    valid_ref[...] = jnp.broadcast_to(row_ref[0:1, here], (LANES, rows)).T
    down_out_ref[:, :length] = jnp.where(inside, down, 0).astype(jnp.int16)
    down_out_ref[:, length:] = jnp.zeros((rows, keys - length), jnp.int16)
    lane_first = lax.broadcasted_iota(jnp.int32, (rows, LANES), 1) < HEAD
    row_first = lax.broadcasted_iota(jnp.int32, (LANES, rows), 0) < HEAD
    for p in range(key.shape[1] // LANES):
        cols = slice(p * LANES, (p + 1) * LANES)
        key_pair, value_pair = key[:, cols], value[:, cols]
        key_turned, value_turned = key_pair.T, value_pair.T
        for u in range(2):
            h = 2 * p + u
            lane_own = lane_first if u == 0 else ~lane_first
            row_own = row_first if u == 0 else ~row_first
            key_ref[h] = jnp.where(lane_own, key_pair, 0.0).astype(bf16)
            value_ref[h] = jnp.where(lane_own, value_pair, 1.0).astype(bf16)
            key_turned_ref[h] = jnp.where(row_own, key_turned, 0.0).astype(bf16)
            value_turned_ref[h] = jnp.where(row_own, value_turned, 0.0).astype(bf16)


def prepare(tokens, weight, bias, buckets, flag, token_mask, expand, row_count, keys, line_count):
    length, depth = tokens.shape
    width = weight.shape[2]
    heads = width // HEAD
    block = 3 * LANES
    row = pl.BlockSpec((block, width), lambda i: (i, 0))
    deep_row = pl.BlockSpec((block, depth), lambda i: (i, 0))
    wide = pl.BlockSpec((heads, block, LANES), lambda i: (0, i, 0))
    turned = pl.BlockSpec((heads, LANES, block), lambda i: (0, 0, i))
    bucket = pl.BlockSpec((block, 1, length), lambda i: (i, 0, 0))
    packed = pl.BlockSpec((block, keys), lambda i: (i, 0))
    wide_shape = jax.ShapeDtypeStruct((heads, keys, LANES), bf16)
    turned_shape = jax.ShapeDtypeStruct((heads, LANES, keys), bf16)
    packed_shape = jax.ShapeDtypeStruct((row_count, keys), jnp.int16)
    return pl.pallas_call(
        partial(prepare_kernel, length=length, line_count=line_count),
        grid=(keys // block,),
        in_specs=[
            deep_row,
            whole_spec(weight),
            whole_spec(bias),
            bucket,
            bucket,
            bucket,
            pl.BlockSpec(memory_space=pltpu.SMEM),
            whole_spec(token_mask),
            pl.BlockSpec(memory_space=pl.ANY),
        ],
        out_specs=[
            row,
            wide,
            turned,
            wide,
            turned,
            deep_row,
            packed,
            packed,
            pl.BlockSpec((block, LANES), lambda i: (i, 0)),
            pl.BlockSpec(memory_space=pl.ANY),
        ],
        out_shape=[
            jax.ShapeDtypeStruct((keys, width), bf16),
            wide_shape,
            turned_shape,
            wide_shape,
            turned_shape,
            jax.ShapeDtypeStruct((keys, depth), bf16),
            packed_shape,
            packed_shape,
            jax.ShapeDtypeStruct((keys, LANES), f32),
            jax.ShapeDtypeStruct((expand.shape[0] // 4, expand.shape[1]), bf16),
        ],
        scratch_shapes=[
            pltpu.VMEM((8, keys), f32),
            pltpu.SemaphoreType.DMA,
            pltpu.SemaphoreType.DMA,
        ],
        compiler_params=pltpu.CompilerParams(
            vmem_limit_bytes=vmem_limit, collective_id=2, has_side_effects=True
        ),
        name="prepare",
    )(
        tokens,
        weight,
        bias,
        *(index.reshape(length, 1, length) for index in buckets),
        flag,
        token_mask,
        expand,
    )


def attend_kernel(
    query_ref,
    key_ref,
    value_ref,
    plane_ref,
    down_ref,
    line_table_ref,
    across_table_ref,
    down_table_ref,
    expand_bias_ref,
    expand_quarter_ref,
    output_ref,
    reduce_ref,
    exp_ref,
    context_ref,
    inverse_ref,
    context_away_ref,
    expand_away_ref,
    output_away_ref,
    reduce_away_ref,
    bias_away_ref,
    score_ref,
    send_ref,
    table_ref,
    bias_ref,
    local_sem,
    send_sem,
    recv_sem,
):
    heads, rows, keys = exp_ref.shape
    step = pl.program_id(0)
    place = lax.axis_index("dp")
    across_mp = {"mp": 1 - lax.axis_index("mp")}
    across = {bit: {"dp": place + bit * (1 - 2 * ((place // bit) % 2))} for bit in (1, 2)}

    def remote(src, dst, n, device):
        return pltpu.make_async_remote_copy(
            src_ref=src,
            dst_ref=dst,
            send_sem=send_sem.at[n],
            recv_sem=recv_sem.at[n],
            device_id=device,
            device_id_type=pl.DeviceIdType.MESH,
        )

    arrays = (
        (expand_quarter_ref, expand_away_ref),
        (output_ref, output_away_ref),
        (reduce_ref, reduce_away_ref),
    )
    quarter = place % 4
    other_chip = (place + 2) % 4
    other_core = quarter + 1 - 2 * (quarter % 2)
    third = (other_core + 2) % 4

    def rows_of(n, which):
        away = arrays[n][1]
        return away.at[quarter_rows(away, which), :]

    def fetch(n):
        ref = arrays[n][0]
        return remote(ref.at[quarter_rows(ref, quarter), :], rows_of(n, quarter), n, across_mp)

    def pass_on(n, stage):
        source = expand_quarter_ref if n == 0 and stage < 2 else rows_of(n, quarter)
        if stage == 0:
            return remote(source, rows_of(n, quarter), 3 + n, across[2])
        if stage == 1:
            return remote(source, rows_of(n, quarter), 6 + n, across[1])
        return remote(rows_of(n, other_chip), rows_of(n, other_chip), 9 + n, across[1])

    def arrival(n, stage):
        region = rows_of(n, (other_chip, other_core, third)[stage])
        return remote(region, region, 3 + 3 * stage + n, across_mp)

    keep = pltpu.make_async_copy(expand_quarter_ref, rows_of(0, quarter), local_sem)
    context_swap = remote(send_ref, context_away_ref, 12, across_mp)
    bias_swap = remote(bias_ref, bias_away_ref, 13, across_mp)

    def event(n, stage):
        if stage == "fetched":
            fetch(n).wait_recv()
            pass_on(n, 0).start()
            pass_on(n, 1).start()
        else:
            arrival(n, 0).wait_recv()
            pass_on(n, 2).start()

    events = {
        (0, 2): ((1, "fetched"),),
        (1, 0): ((0, "passed"), (2, "fetched")),
        (1, 1): ((1, "passed"),),
    }

    @pl.when(step == 0)
    def _():
        barrier = pltpu.get_barrier_semaphore()
        for device in (across_mp, across[1], across[2]):
            pl.semaphore_signal(
                barrier, inc=1, device_id=device, device_id_type=pl.DeviceIdType.MESH
            )
        pl.semaphore_wait(barrier, 3)
        bias_ref[...] = jnp.broadcast_to(
            expand_bias_ref[...].astype(f32).reshape(1, -1), bias_ref.shape
        )
        bias_swap.start()
        for t, ref in enumerate((line_table_ref, across_table_ref, down_table_ref)):
            count = ref.shape[1]
            lanes = jnp.concatenate(
                [ref[...].astype(f32), jnp.full((heads, LANES - count), large_negative, f32)], axis=1
            )
            for h in range(heads):
                table_ref[t * heads + h] = jnp.broadcast_to(lanes[h : h + 1], (STRIP, LANES)).astype(
                    bf16
                )
        fetch(1).start()
        fetch(2).start()
        pass_on(0, 0).start()
        pass_on(0, 1).start()
        keep.start()

    for h in range(heads):
        pair = slice(h // 2 * LANES, (h // 2 + 1) * LANES)
        score_ref[h] = dot_f32(query_ref[:, pair], key_ref[h])

    lanes = [slice(c * LANES, (c + 1) * LANES) for c in range(keys // LANES)]

    def scores_of(at):
        scores = [[] for _ in range(heads)]
        for cols in lanes:
            packed = plane_ref[at, cols]
            bias = [None] * heads
            for t, index in enumerate(
                (packed & jnp.int16(255), packed >> jnp.int16(8), down_ref[at, cols])
            ):
                for h in range(heads):
                    found = gather_lanes(table_ref[t * heads + h], index).astype(f32)
                    bias[h] = found if t == 0 else bias[h] + found
            for h in range(heads):
                scores[h].append(score_ref[h, at, cols] + bias[h])
        return scores

    def exps_of(scores):
        exps = []
        for parts in scores:
            top = parts[0]
            for part in parts[1:]:
                top = jnp.maximum(top, part)
            top = jnp.max(top, axis=1, keepdims=True)
            exps.append([jnp.exp(part - top).astype(bf16) for part in parts])
        return exps

    def strips(n, carry):
        for (at_step, at_turn), pieces in events.items():

            @pl.when((step == at_step) & (n == at_turn))
            def _():
                for piece in pieces:
                    event(*piece)

        start = pl.multiple_of(n * ATTEND_STRIPS * STRIP, STRIP)
        places = [pl.ds(start + k * STRIP, STRIP) for k in range(ATTEND_STRIPS)]
        scores = [scores_of(at) for at in places]
        exps = [exps_of(part) for part in scores]
        for at, part in zip(places, exps):
            for h in range(heads):
                for c, cols in enumerate(lanes):
                    exp_ref[h, at, cols] = part[h][c]
        return carry

    lax.fori_loop(0, rows // (ATTEND_STRIPS * STRIP), strips, 0)
    first = lax.broadcasted_iota(jnp.int32, (rows, LANES), 1) < HEAD
    for p in range(heads // 2):
        cols = slice(p * LANES, (p + 1) * LANES)
        even = dot_f32(exp_ref[2 * p], value_ref[2 * p])
        odd = dot_f32(exp_ref[2 * p + 1], value_ref[2 * p + 1])
        sums = jnp.where(first, pltpu.roll(even, HEAD, 1), pltpu.roll(odd, HEAD, 1))
        inverse = 1.0 / sums
        inverse_ref[:, cols] = inverse
        context = (jnp.where(first, even, odd) * inverse).astype(bf16)
        context_ref[:, cols] = context

        @pl.when(step == 0)
        def _():
            send_ref[:, cols] = context

    pl.when(step == 0)(context_swap.start)

    @pl.when(step == 1)
    def _():
        event(2, "passed")
        keep.wait()
        context_swap.wait()
        bias_swap.wait()
        for n in range(3):
            arrival(n, 1).wait_recv()
            arrival(n, 2).wait_recv()
            for stage in range(3):
                pass_on(n, stage).wait_send()
        fetch(1).wait_send()
        fetch(2).wait_send()


def attend(
    query,
    key_turned,
    value_ones,
    plane,
    down,
    tables,
    expand_bias,
    expand_quarter,
    output,
    reduce,
):
    heads, _, keys = key_turned.shape
    row_count = plane.shape[0]
    width = heads * HEAD
    half_rows = row_count // 2

    def half(i):
        return lax.rem(i + 1 - lax.axis_index("mp"), 2)

    anywhere = pl.BlockSpec(memory_space=pl.ANY)
    index_spec = pl.BlockSpec((half_rows, keys), lambda i: (half(i), 0))
    row_spec = pl.BlockSpec((half_rows, width), lambda i: (half(i), 0))
    return pl.pallas_call(
        attend_kernel,
        grid=(2,),
        in_specs=[
            row_spec,
            whole_spec(key_turned),
            whole_spec(value_ones),
            index_spec,
            index_spec,
            *(whole_spec(table) for table in tables),
            whole_spec(expand_bias),
            anywhere,
            anywhere,
            anywhere,
        ],
        out_specs=[
            pl.BlockSpec((heads, half_rows, keys), lambda i: (0, half(i), 0)),
            row_spec,
            row_spec,
            anywhere,
            anywhere,
            anywhere,
            anywhere,
            anywhere,
        ],
        out_shape=[
            jax.ShapeDtypeStruct((heads, row_count, keys), bf16),
            jax.ShapeDtypeStruct((row_count, width), bf16),
            jax.ShapeDtypeStruct((row_count, width), f32),
            jax.ShapeDtypeStruct((half_rows, width), bf16),
            jax.ShapeDtypeStruct((4 * expand_quarter.shape[0], expand_quarter.shape[1]), bf16),
            jax.ShapeDtypeStruct(output.shape, bf16),
            jax.ShapeDtypeStruct(reduce.shape, bf16),
            jax.ShapeDtypeStruct((8, expand_bias.size), f32),
        ],
        scratch_shapes=[
            pltpu.VMEM((heads, half_rows, keys), f32),
            pltpu.VMEM((half_rows, width), bf16),
            pltpu.VMEM((3 * heads, STRIP, LANES), bf16),
            pltpu.VMEM((8, expand_bias.size), f32),
            pltpu.SemaphoreType.DMA,
            pltpu.SemaphoreType.DMA((14,)),
            pltpu.SemaphoreType.DMA((14,)),
        ],
        compiler_params=pltpu.CompilerParams(
            vmem_limit_bytes=vmem_limit, collective_id=1, has_side_effects=True
        ),
        name="attend",
    )(
        query,
        key_turned,
        value_ones,
        plane,
        down,
        *tables,
        expand_bias,
        expand_quarter,
        output,
        reduce,
    )


def attend_back_kernel(
    exp_ref,
    grad_ref,
    context_ref,
    query_ref,
    value_ref,
    key_ref,
    grad_score_ref,
    grad_query_ref,
    grad_key_ref,
    grad_value_ref,
):
    heads, rows, _ = exp_ref.shape

    @pl.when(pl.program_id(0) == 0)
    def _():
        grad_key_ref[...] = jnp.zeros_like(grad_key_ref)
        grad_value_ref[...] = jnp.zeros_like(grad_value_ref)

    first = lax.broadcasted_iota(jnp.int32, (rows, LANES), 1) < HEAD
    for p in range(heads // 2):
        cols = slice(p * LANES, (p + 1) * LANES)
        grad = grad_ref[:, cols]
        product = grad.astype(f32) * context_ref[:, cols].astype(f32)
        query_turned = query_ref[:, cols].T
        grad_turned = grad.T
        grad_query = None
        for u in range(2):
            h = 2 * p + u
            half = slice(u * HEAD, (u + 1) * HEAD)
            own = first if u == 0 else ~first
            total = jnp.sum(jnp.where(own, product, 0.0), axis=1, keepdims=True)
            grad_exp = dot_f32(grad, value_ref[h])
            grad_score = (exp_ref[h].astype(f32) * (grad_exp - total)).astype(bf16)
            grad_score_ref[h] = grad_score
            part = dot_f32(grad_score, key_ref[h])
            grad_query = part if u == 0 else grad_query + part
            grad_key_ref[h] += dot_f32(query_turned[half], grad_score)
            grad_value_ref[h] += dot_f32(grad_turned[half], exp_ref[h])
        grad_query_ref[:, cols] = (grad_query * 0.125).astype(bf16)


def attend_back(exps, grad, context, query, value_turned, key_wide):
    heads, row_count, keys = exps.shape
    width = heads * HEAD
    row_spec = pl.BlockSpec((BLOCK_ROWS, width), lambda i: (i, 0))
    exp_spec = pl.BlockSpec((heads, BLOCK_ROWS, keys), lambda i: (0, i, 0))
    sum_spec = pl.BlockSpec((heads, HEAD, keys), lambda i: (0, 0, 0))
    return pl.pallas_call(
        attend_back_kernel,
        grid=(row_count // BLOCK_ROWS,),
        in_specs=[
            exp_spec,
            row_spec,
            row_spec,
            row_spec,
            whole_spec(value_turned),
            whole_spec(key_wide),
        ],
        out_specs=[exp_spec, row_spec, sum_spec, sum_spec],
        out_shape=[
            jax.ShapeDtypeStruct((heads, row_count, keys), bf16),
            jax.ShapeDtypeStruct((row_count, width), bf16),
            jax.ShapeDtypeStruct((heads, HEAD, keys), f32),
            jax.ShapeDtypeStruct((heads, HEAD, keys), f32),
        ],
        compiler_params=pltpu.CompilerParams(vmem_limit_bytes=vmem_limit),
        name="attend_back",
    )(exps, grad, context, query, value_turned, key_wide)


def table_strips(strips, sum_ref, heads, keys, high_counts):
    base = 0
    for t in range(3):
        shift = 8 if t == 1 else 0
        highs, lows = [], []
        for grad_of, plane_of, down_of in strips:
            for c in range(keys // LANES):
                cols = slice(c * LANES, (c + 1) * LANES)
                index = down_of(cols) if t == 2 else plane_of(cols)
                low = index & jnp.int16(15 << shift)
                high = index & jnp.int16(48 << shift)
                lows.append(
                    jnp.concatenate(
                        [
                            jnp.where(low == jnp.int16(x << shift), bf16(1), bf16(0))
                            for x in range(16)
                        ]
                    )
                )
                parts = []
                for x in range(high_counts[t]):
                    mask = high == jnp.int16(x << (4 + shift))
                    parts += [jnp.where(mask, grad_of(h, cols), bf16(0)) for h in range(heads)]
                highs.append(jnp.concatenate(parts))
        span = slice(base, base + high_counts[t] * heads * STRIP)
        sum_ref[span, :] += lax.dot_general(
            jnp.concatenate(highs, axis=1),
            jnp.concatenate(lows, axis=1),
            (((1,), (1,)), ((), ())),
            preferred_element_type=f32,
        )
        base = span.stop


def table_finish(sum_ref, out_ref, count):
    row_of_lane = lax.broadcasted_iota(jnp.int32, (STRIP, 16 * STRIP), 1) % STRIP
    same = row_of_lane == lax.broadcasted_iota(jnp.int32, (STRIP, 16 * STRIP), 0)
    for o in range(count):
        block = sum_ref[o * STRIP : (o + 1) * STRIP, :]
        out_ref[o : o + 1, :] = jnp.sum(jnp.where(same, block, 0.0), axis=0, keepdims=True)


def table_result(out, high_counts, heads):
    summed = jnp.sum(out.reshape(sum(high_counts), heads, 16, STRIP), axis=-1)
    return summed.transpose(0, 2, 1).reshape(-1, heads)


def table_kernel(grad_score_ref, plane_ref, down_ref, out_ref, sum_ref, *, high_counts):
    heads, rows, keys = grad_score_ref.shape
    step = pl.program_id(0)

    @pl.when(step == 0)
    def _():
        sum_ref[...] = jnp.zeros_like(sum_ref)

    def refs_at(start):
        at = pl.ds(pl.multiple_of(start, STRIP), STRIP)
        return (
            lambda h, cols: grad_score_ref[h, at, cols],
            lambda cols: plane_ref[at, cols],
            lambda cols: down_ref[at, cols],
        )

    def strips(r, carry):
        start = r * (TABLE_STRIPS * STRIP)
        table_strips(
            [refs_at(start + k * STRIP) for k in range(TABLE_STRIPS)],
            sum_ref,
            heads,
            keys,
            high_counts,
        )
        return carry

    lax.fori_loop(0, rows // (TABLE_STRIPS * STRIP), strips, 0)

    @pl.when(step == pl.num_programs(0) - 1)
    def _():
        table_finish(sum_ref, out_ref, out_ref.shape[0])


def table_sums(grad_scores, plane, down, counts):
    heads, row_count, keys = grad_scores.shape
    high_counts = (counts[0] // 16, counts[1] // 16, counts[1] // 16)
    high_rows = sum(high_counts) * heads
    index_spec = pl.BlockSpec((BLOCK_ROWS, keys), lambda i: (i, 0))
    out = pl.pallas_call(
        partial(table_kernel, high_counts=high_counts),
        grid=(row_count // BLOCK_ROWS,),
        in_specs=[
            pl.BlockSpec((heads, BLOCK_ROWS, keys), lambda i: (0, i, 0)),
            index_spec,
            index_spec,
        ],
        out_specs=pl.BlockSpec((high_rows, 16 * STRIP), lambda i: (0, 0)),
        out_shape=jax.ShapeDtypeStruct((high_rows, 16 * STRIP), f32),
        scratch_shapes=[pltpu.VMEM((high_rows * STRIP, 16 * STRIP), f32)],
        compiler_params=pltpu.CompilerParams(vmem_limit_bytes=vmem_limit),
        name="table_sums",
    )(grad_scores, plane, down)
    return table_result(out, high_counts, heads)


CHUNK = 768
CHUNKS = 6
LOCAL_CHUNKS = 2
PARTS = (CHUNK // 2, CHUNK // 4, CHUNK // 8, CHUNK // 16)
BITS = ((1, 2, 4, 8), (1, 4, 2, 8), (1, 2, 4, 8), (1, 4, 2, 8), (1, 2, 4, 8), (1, 4, 2, 8))
BACK_ROWS = 112
EXCHANGE = (
    ("b", 0, 0, 2), ("b", 0, 0, 3), ("b", 0, 0, 4), ("b", 1, 0, 5), ("b", 4, 1, 2), ("b", 6, 1, 3),
    ("b", 8, 1, 4), ("b", 9, 1, 5), ("b", 20, 2, 2), ("b", 22, 2, 3), ("p", 0, 3, 2), ("p", 2, 2, 4),
    ("p", 3, 2, 5), ("p", 3, 3, 3), ("p", 3, 0, 0), ("p", 3, 0, 1), ("t", 0, 4, 2), ("t", 1, 1, 0),
    ("t", 1, 1, 1), ("t", 2, 4, 3), ("t", 2, "small", 0), ("t", 3, 3, 4), ("t", 4, 5, 2),
    ("t", 5, "send", 0), ("t", 6, 3, 5), ("t", 6, 2, 0), ("t", 6, 2, 1), ("t", 6, "small", 1),
    ("t", 8, 5, 3), ("t", 9, 4, 4), ("t", 10, 4, 5), ("t", 11, 6, 2), ("t", 11, "small", 2),
    ("t", 12, 3, 1), ("t", 12, 3, 0), ("t", 13, 6, 3), ("t", 15, 5, 4), ("t", 16, "layer", 0),
    ("t", 16, "small", 3), ("t", 17, 5, 5), ("t", 17, 7, 3), ("t", 18, 7, 2), ("t", 18, "input", 0),
    ("t", 19, 4, 1), ("t", 19, 4, 0), ("t", 20, "small", 4), ("t", 21, 6, 4), ("t", 22, 8, 2),
    ("t", 23, 6, 5), ("t", 24, 9, 2), ("t", 25, "small", 5), ("t", 26, 8, 3), ("t", 27, 5, 1),
    ("t", 27, 7, 5), ("t", 28, 9, 3), ("t", 29, 5, 0), ("t", 29, 7, 4), ("t", 31, 6, 1),
    ("t", 33, 8, 5), ("e", 0, 9, 5), ("e", 0, 8, 4), ("e", 0, 6, 0), ("e", 0, 9, 4), ("e", 0, 7, 1),
    ("e", 0, 8, 1), ("e", 0, 7, 0), ("e", 0, 8, 0),
)


def plan_slots(phase, count):
    slots = [[] for _ in range(count)]
    for name, at, event, which in EXCHANGE:
        if name == phase:
            slots[at].append((event, which))
    return slots


def finish_kernel(
    exp_ref,
    inverse_ref,
    plane_ref,
    down_ref,
    context_ref,
    query_ref,
    token_ref,
    grad_ref,
    layer_ref,
    value_ref,
    key_ref,
    project_ref,
    output_ref,
    expand_ref,
    expand_away_ref,
    reduce_ref,
    reduce_away_ref,
    small_ref,
    total_ref,
    layer_out_ref,
    input_ref,
    small_out_ref,
    table_ref,
    score_ref,
    output_buf,
    grad_buf,
    value_buf,
    key_buf,
    context_buf,
    query_buf,
    token_buf,
    project_buf,
    ring_buf,
    inverse_buf,
    grad_key_buf,
    grad_value_buf,
    triple_buf,
    input_send_buf,
    input_recv_buf,
    input_buf,
    plane_buf,
    down_buf,
    sum_ref,
    own_buf,
    away_buf,
    core_buf,
    core_away_buf,
    first_buf,
    first_away_buf,
    y_buf,
    second_buf,
    third_buf,
    small_buf,
    small_recv_buf,
    table_buf,
    table_recv_buf,
    resident_sem,
    block_sem,
    ring_sem,
    load_sem,
    local_sem,
    out_sem,
    send_sem,
    recv_sem,
    wide_send_sem,
    wide_recv_sem,
    small_send_sem,
    small_recv_sem,
    table_send_sem,
    table_recv_sem,
    *,
    high_counts,
):
    heads, row_count, keys = exp_ref.shape
    width = heads * HEAD
    half_rows = row_count // 2
    rows = BACK_ROWS
    blocks = row_count // rows
    block_strips = rows // STRIP
    turns = row_count // (TABLE_STRIPS * STRIP)
    place = lax.axis_index("dp")
    mp_index = lax.axis_index("mp")
    side_of = {bit: (place // bit) % 2 for bit in (1, 2, 4, 8)}
    partner_of = {bit: {"dp": place + bit * (1 - 2 * side_of[bit])} for bit in (1, 2, 4, 8)}
    across_mp = {"mp": 1 - mp_index}

    barrier = pltpu.get_barrier_semaphore()
    for device in (*partner_of.values(), across_mp):
        pl.semaphore_signal(barrier, inc=1, device_id=device, device_id_type=pl.DeviceIdType.MESH)
    pl.semaphore_wait(barrier, 5)

    def rows_at(start, size):
        return pl.ds(pl.multiple_of(start, STRIP), size)

    def remote(src, dst, send, recv, device):
        return pltpu.make_async_remote_copy(
            src_ref=src,
            dst_ref=dst,
            send_sem=send,
            recv_sem=recv,
            device_id=device,
            device_id_type=pl.DeviceIdType.MESH,
        )

    mine = rows_at(mp_index * half_rows, half_rows)
    others = rows_at((1 - mp_index) * half_rows, half_rows)
    grad_swap = remote(
        grad_ref, grad_buf.at[1], wide_send_sem.at[0], wide_recv_sem.at[0], across_mp
    )
    input_swap = remote(
        input_send_buf, input_recv_buf, wide_send_sem.at[1], wide_recv_sem.at[1], across_mp
    )
    layer_swap = remote(
        layer_ref, layer_out_ref.at[mine, :], wide_send_sem.at[2], wide_recv_sem.at[2], across_mp
    )
    layer_arrival = remote(
        layer_out_ref.at[others, :],
        layer_out_ref.at[others, :],
        wide_send_sem.at[2],
        wide_recv_sem.at[2],
        across_mp,
    )
    layer_keep = pltpu.make_async_copy(layer_ref, layer_out_ref.at[mine, :], out_sem.at[2])
    grad_swap.start()

    residents = [
        pltpu.make_async_copy(src, dst, resident_sem.at[n])
        for n, (src, dst) in enumerate(
            (
                (grad_ref, grad_buf.at[0]),
                (output_ref, output_buf),
                (context_ref, context_buf),
                (query_ref, query_buf),
                (value_ref, value_buf),
                (key_ref, key_buf),
                (small_ref, small_buf.at[0]),
                (token_ref, token_buf),
                (project_ref, project_buf),
            )
        )
    ]

    def block_rows(block):
        start = (mp_index * (blocks // 2) + block) % blocks
        return rows_at(start * rows, rows)

    def block_copies(block, slot):
        at = block_rows(block)
        return (
            pltpu.make_async_copy(exp_ref.at[:, at, :], ring_buf.at[slot], block_sem.at[slot, 0]),
            pltpu.make_async_copy(inverse_ref.at[at, :], inverse_buf.at[slot], block_sem.at[slot, 1]),
        )

    def score_copy(block, slot):
        return pltpu.make_async_copy(
            ring_buf.at[2 + slot], score_ref.at[:, block_rows(block), :], out_sem.at[slot]
        )

    def ring_copies(block):
        slot = block % 4
        at = rows_at(block * rows, rows)
        return (
            pltpu.make_async_copy(score_ref.at[:, at, :], ring_buf.at[slot], ring_sem.at[slot, 0]),
            pltpu.make_async_copy(plane_ref.at[at, :], plane_buf.at[slot], ring_sem.at[slot, 1]),
            pltpu.make_async_copy(down_ref.at[at, :], down_buf.at[slot], ring_sem.at[slot, 2]),
        )

    def is_away(chunk):
        return chunk >= LOCAL_CHUNKS

    loads = {}
    for ref, away_ref, wide in (
        (expand_ref, expand_away_ref, True),
        (reduce_ref, reduce_away_ref, False),
    ):
        for k in range(2):
            piece = slice(k * CHUNK, (k + 1) * CHUNK)
            index = (slice(None), piece) if wide else (piece, slice(None))
            chunk = LOCAL_CHUNKS + len(loads)
            loads[chunk] = (
                pltpu.make_async_copy(ref.at[index], own_buf.at[chunk], load_sem.at[chunk, 0]),
                pltpu.make_async_copy(
                    away_ref.at[index], away_buf.at[chunk - LOCAL_CHUNKS], load_sem.at[chunk, 1]
                ),
            )

    for copy in loads[LOCAL_CHUNKS]:
        copy.start()
    for copy in residents[:2]:
        copy.start()
    for copy in block_copies(0, 0):
        copy.start()
    for copy in residents[2:6]:
        copy.start()
    for chunk in range(LOCAL_CHUNKS + 1, CHUNKS):
        for copy in loads[chunk]:
            copy.start()
    residents[6].start()
    for copy in residents[7:]:
        copy.start()

    keeps, leaves = [], []
    for bits in BITS:
        kept, left, base = [], [], 0
        for size, bit in zip(PARTS, bits):
            kept.append(base + side_of[bit] * size)
            left.append(base + (1 - side_of[bit]) * size)
            base = base + side_of[bit] * size
        keeps.append(kept)
        leaves.append(left)
    arrivals = (core_buf, first_buf, second_buf, third_buf)
    away_arrivals = (core_away_buf, first_away_buf)

    def staged(src, dst, chunk, stage, device):
        return remote(src, dst, send_sem.at[chunk, stage], recv_sem.at[chunk, stage], device)

    def scatter(chunk, level):
        return staged(
            own_buf.at[chunk, rows_at(leaves[chunk][level], PARTS[level]), :],
            arrivals[level].at[chunk],
            chunk,
            level,
            partner_of[BITS[chunk][level]],
        )

    def scatter_away(chunk, level):
        return staged(
            away_buf.at[chunk - LOCAL_CHUNKS, rows_at(leaves[chunk][level], PARTS[level]), :],
            away_arrivals[level].at[chunk - LOCAL_CHUNKS],
            chunk,
            4 + level,
            partner_of[BITS[chunk][level]],
        )

    def hand_over(chunk):
        return staged(
            away_buf.at[chunk - LOCAL_CHUNKS, rows_at(keeps[chunk][1], PARTS[1]), :],
            y_buf.at[chunk - LOCAL_CHUNKS],
            chunk,
            6,
            across_mp,
        )

    def total_rows(chunk, start, size):
        return total_ref.at[rows_at(chunk * CHUNK + start, size), :]

    def gather(chunk, level):
        kept, size = keeps[chunk][level], PARTS[level]
        if level == 3:
            src = own_buf.at[chunk, rows_at(kept, size), :]
        else:
            src = total_rows(chunk, kept, size)
        return staged(
            src, total_rows(chunk, kept, size), chunk, 7 + level, partner_of[BITS[chunk][level]]
        )

    def gathered(chunk, level):
        region = total_rows(chunk, leaves[chunk][level], PARTS[level])
        return staged(region, region, chunk, 7 + level, partner_of[BITS[chunk][level]])

    def store_own(chunk):
        return pltpu.make_async_copy(
            own_buf.at[chunk, rows_at(keeps[chunk][3], PARTS[3]), :],
            total_rows(chunk, keeps[chunk][3], PARTS[3]),
            local_sem.at[chunk],
        )

    def add(buf, chunk, start, size, arrived):
        piece = PARTS[3]

        def step(n, carry):
            here = rows_at(start + n * piece, piece)
            there = rows_at(n * piece, piece)
            buf[chunk, here, :] = buf[chunk, here, :] + arrived[there, :]
            return carry

        lax.fori_loop(0, size // piece, step, 0)

    def add_level(chunk, level):
        scatter(chunk, level).wait_recv()
        add(own_buf, chunk, keeps[chunk][level], PARTS[level], arrivals[level].at[chunk])

    def add_level_away(chunk, level):
        at = chunk - LOCAL_CHUNKS
        scatter_away(chunk, level).wait_recv()
        add(away_buf, at, keeps[chunk][level], PARTS[level], away_arrivals[level].at[at])

    def exchange(event, chunk):
        away = is_away(chunk)
        if event == 0:
            if away:
                for copy in loads[chunk]:
                    copy.wait()
                scatter_away(chunk, 0).start()
            scatter(chunk, 0).start()
            return
        if event == 1:
            if away:
                add_level_away(chunk, 0)
                scatter_away(chunk, 1).start()
            add_level(chunk, 0)
            scatter(chunk, 1).start()
            return
        if away and event == 2:
            add_level_away(chunk, 1)
            hand_over(chunk).start()
            add_level(chunk, 1)
            return
        if away:
            event -= 1
            if event == 2:
                hand_over(chunk).wait_recv()
                add(own_buf, chunk, keeps[chunk][1], PARTS[1], y_buf.at[chunk - LOCAL_CHUNKS])
        elif event == 2:
            add_level(chunk, 1)
        if event == 2:
            scatter(chunk, 2).start()
        elif event == 3:
            add_level(chunk, 2)
            scatter(chunk, 3).start()
        elif event == 4:
            add_level(chunk, 3)
            store_own(chunk).start()
            gather(chunk, 3).start()
        else:
            level = 8 - event
            if level == 3:
                store_own(chunk).wait()
            gathered(chunk, level).wait_recv()
            if level > 0:
                gather(chunk, level - 1).start()

    small_devices = (across_mp, *partner_of.values())

    def small_hop(n):
        return remote(
            small_buf.at[n],
            small_recv_buf.at[n],
            small_send_sem.at[n],
            small_recv_sem.at[n],
            small_devices[n],
        )

    def small_step(n):
        if n == 0:
            residents[6].wait()
        else:
            small_hop(n - 1).wait_recv()
            small_buf[n] = small_buf[n - 1] + small_recv_buf[n - 1]
        if n < 5:
            small_hop(n).start()
        else:
            small_out_ref[...] = small_buf[n]

    def input_rows(side):
        return mine if side == 0 else others

    def input_product(side, target):
        at = input_rows(side)
        part = None
        for k in range(3):
            product = lax.dot_general(
                triple_buf[k, at, :],
                project_buf[k, rows_at(target * width, width), :],
                (((1,), (1,)), ((), ())),
                preferred_element_type=f32,
            )
            part = product if part is None else part + product
        if side == 0:
            cols = pl.ds(pl.multiple_of(target * width, LANES), width)
            part = part + grad_buf[0, :, cols].astype(f32)
        return part

    def input_store(side):
        return pltpu.make_async_copy(
            input_buf.at[side], input_ref.at[input_rows(side), :], out_sem.at[3 + side]
        )

    def run(event, which):
        if event == "small":
            small_step(which)
        elif event == "send":
            input_swap.start()
        elif event == "layer":
            layer_swap.start()
            layer_keep.start()
        elif event == "input":
            input_swap.wait_recv()
            for side in range(2):
                part = input_product(side, mp_index)
                input_buf[side] = part + input_recv_buf[input_rows(side), :].astype(f32)
                input_store(side).start()
        else:
            exchange(event, which)

    pairs = heads // 2
    block_slots = plan_slots("b", blocks * pairs)
    part_slots = plan_slots("p", 4)
    turn_slots = plan_slots("t", turns)
    rest = plan_slots("e", 1)[0]

    def run_all(steps):
        for event, which in steps:
            run(event, which)

    def dispatch(slots, n, low, high):
        if not any(slots[low:high]):
            return
        if high - low == 1:
            for event, which in slots[low]:
                run(event, which)
            return
        middle = (low + high) // 2
        if any(slots[low:middle]):
            pl.when(n < middle)(lambda: dispatch(slots, n, low, middle))
        if any(slots[middle:high]):
            pl.when(n >= middle)(lambda: dispatch(slots, n, middle, high))

    grad_key_buf[...] = jnp.zeros_like(grad_key_buf)
    grad_value_buf[...] = jnp.zeros_like(grad_value_buf)
    sum_ref[...] = jnp.zeros_like(sum_ref)
    for copy in residents[:6]:
        copy.wait()
    first = lax.broadcasted_iota(jnp.int32, (rows, LANES), 1) < HEAD

    def back(block, carry):
        slot = block % 2
        at = block_rows(block)
        for copy in block_copies(block, slot):
            copy.wait()

        @pl.when(block + 1 < blocks)
        def _():
            for copy in block_copies(block + 1, 1 - slot):
                copy.start()

        pl.when(block == blocks // 2)(grad_swap.wait_recv)
        pl.when(block >= 2)(lambda: score_copy(block - 2, slot).wait())
        side = block // (blocks // 2)
        local = rows_at((block % (blocks // 2)) * rows, rows)
        grad_context = lax.dot_general(
            grad_buf[side, local, :],
            output_buf[...],
            (((1,), (1,)), ((), ())),
            preferred_element_type=f32,
        )
        scaled = (grad_context * inverse_buf[slot]).astype(bf16)
        for p in range(pairs):
            dispatch(block_slots, block * pairs + p, 0, blocks * pairs)
            cols = slice(p * LANES, (p + 1) * LANES)
            grad = scaled[:, cols]
            product = grad.astype(f32) * context_buf[at, cols].astype(f32)
            query_turned = query_buf[at, cols].T
            grad_turned = grad.T
            grad_query = None
            for u in range(2):
                h = 2 * p + u
                half = slice(u * HEAD, (u + 1) * HEAD)
                own = first if u == 0 else ~first
                total = jnp.sum(jnp.where(own, product, 0.0), axis=1, keepdims=True)
                exps = ring_buf[slot, h]
                grad_exp = dot_f32(grad, value_buf[h])
                grad_score = (exps.astype(f32) * (grad_exp - total)).astype(bf16)
                ring_buf[2 + slot, h] = grad_score
                part = dot_f32(grad_score, key_buf[h])
                grad_query = part if u == 0 else grad_query + part
                grad_key_buf[h] += dot_f32(query_turned[half], grad_score)
                grad_value_buf[h] += dot_f32(grad_turned[half], exps)
            triple_buf[0, at, cols] = (grad_query * 0.125).astype(bf16)
        score_copy(block, slot).start()
        return carry

    lax.fori_loop(0, blocks, back, 0)

    score_copy(blocks - 2, blocks % 2).wait()
    score_copy(blocks - 1, (blocks - 1) % 2).wait()
    for block in range(2):
        for copy in ring_copies(block):
            copy.start()
    run_all(part_slots[0])
    triple_buf[0, row_count:keys, :] = jnp.zeros((keys - row_count, width), bf16)
    for k, ref in ((1, grad_key_buf), (2, grad_value_buf)):
        for h in range(0, heads, 2):
            pair = ref[h : h + 2].reshape(LANES, keys)
            triple_buf[k, :, h * HEAD : (h + 2) * HEAD] = pair.T.astype(bf16)
    run_all(part_slots[1])
    for copy in residents[7:]:
        copy.wait()
    tokens_in = (((0,), (0,)), ((), ()))
    places = ((0, 0), (0, width), (1, 0))
    for k, (chunk, start) in enumerate(places):
        own_buf[chunk, start : start + width, :] = lax.dot_general(
            triple_buf[k], token_buf[...], tokens_in, preferred_element_type=f32
        ).astype(bf16)
    run_all(part_slots[2])
    own_buf[1, width : 2 * width, :] = (
        lax.dot_general(
            context_buf[mine, :], grad_buf[0], tokens_in, preferred_element_type=f32
        )
        + lax.dot_general(
            context_buf[others, :], grad_buf[1], tokens_in, preferred_element_type=f32
        )
    ).astype(bf16)
    run_all(part_slots[3])
    for side in range(2):
        input_send_buf[input_rows(side), :] = input_product(side, 1 - mp_index).astype(bf16)
    biases = jnp.concatenate(
        [
            jnp.sum(triple_buf[0].astype(f32), axis=0, keepdims=True),
            jnp.sum(triple_buf[2].astype(f32), axis=0, keepdims=True),
        ],
        axis=1,
    )

    def turn(n, carry):
        last = n * TABLE_STRIPS + TABLE_STRIPS - 1
        block = last // block_strips

        @pl.when(last % block_strips < TABLE_STRIPS)
        def _():
            for copy in ring_copies(block):
                copy.wait()

            @pl.when(block + 2 < blocks)
            def _():
                for copy in ring_copies(block + 2):
                    copy.start()

        dispatch(turn_slots, n, 0, turns)

        def refs_at(strip):
            slot = (strip // block_strips) % 4
            at = rows_at((strip % block_strips) * STRIP, STRIP)
            return (
                lambda h, cols: ring_buf[slot, h, at, cols],
                lambda cols: plane_buf[slot, at, cols],
                lambda cols: down_buf[slot, at, cols],
            )

        table_strips(
            [refs_at(n * TABLE_STRIPS + k) for k in range(TABLE_STRIPS)],
            sum_ref,
            heads,
            keys,
            high_counts,
        )
        return carry

    lax.fori_loop(0, turns, turn, 0)

    table_rows = sum(high_counts) * heads
    table_finish(sum_ref, table_buf.at[0], table_rows)
    lanes = table_buf.shape[2]
    pieces = 2 * width // lanes
    for n in range(pieces):
        table_buf[0, table_rows + n : table_rows + n + 1, :] = biases[:, n * lanes : (n + 1) * lanes]
    spare = table_buf.shape[1] - table_rows - pieces
    table_buf[0, table_rows + pieces :, :] = jnp.zeros((spare, lanes), f32)
    table_devices = tuple(partner_of.values())

    def table_hop(n):
        return remote(
            table_buf.at[n],
            table_recv_buf.at[n],
            table_send_sem.at[n],
            table_recv_sem.at[n],
            table_devices[n],
        )

    def table_step(n):
        if n > 0:
            table_hop(n - 1).wait_recv()
            table_buf[n] = table_buf[n - 1] + table_recv_buf[n - 1]
        if n < 4:
            table_hop(n).start()

    table_step(0)
    for n, (event, which) in enumerate(rest):
        if n % 3 == 2 and n // 3 < 4:
            table_step(n // 3 + 1)
        run(event, which)
    for n in range(min(len(rest) // 3, 4), 4):
        table_step(n + 1)
    table_ref[...] = table_buf[4]

    layer_arrival.wait_recv()
    layer_keep.wait()
    grad_swap.wait_send()
    input_swap.wait_send()
    layer_swap.wait_send()
    for side in range(2):
        input_store(side).wait()
    for n in range(5):
        small_hop(n).wait_send()
    for n in range(4):
        table_hop(n).wait_send()
    for chunk in range(CHUNKS):
        for level in range(4):
            scatter(chunk, level).wait_send()
            gather(chunk, level).wait_send()
        if is_away(chunk):
            scatter_away(chunk, 0).wait_send()
            scatter_away(chunk, 1).wait_send()
            hand_over(chunk).wait_send()


def finish(
    exps,
    inverse,
    plane,
    down,
    context,
    query,
    tokens,
    grad,
    layer,
    value_turned,
    key_wide,
    project_weight,
    output_weight,
    expand,
    reduce,
    small,
    counts,
):
    heads, row_count, keys = exps.shape
    width = heads * HEAD
    depth = tokens.shape[1]
    half_rows = row_count // 2
    high_counts = (counts[0] // 16, counts[1] // 16, counts[1] // 16)
    high_rows = sum(high_counts) * heads
    low_lanes = 16 * STRIP
    table_shape = (round_up(high_rows + 2 * width // low_lanes, 8), low_lanes)
    away = CHUNKS - LOCAL_CHUNKS
    anywhere = pl.BlockSpec(memory_space=pl.ANY)
    in_vmem = pl.BlockSpec(memory_space=pltpu.VMEM)
    dma = pltpu.SemaphoreType.DMA
    total, layer_full, input_full, small_sum, table_sum, _ = pl.pallas_call(
        partial(finish_kernel, high_counts=high_counts),
        in_specs=[anywhere] * 18,
        out_specs=[anywhere, anywhere, anywhere, in_vmem, in_vmem, anywhere],
        out_shape=[
            jax.ShapeDtypeStruct((CHUNKS * CHUNK, CHUNK), bf16),
            jax.ShapeDtypeStruct((row_count, depth), bf16),
            jax.ShapeDtypeStruct((row_count, width), f32),
            jax.ShapeDtypeStruct(small.shape, f32),
            jax.ShapeDtypeStruct(table_shape, f32),
            jax.ShapeDtypeStruct(exps.shape, bf16),
        ],
        scratch_shapes=[
            pltpu.VMEM(output_weight.shape, bf16),
            pltpu.VMEM((2, half_rows, depth), bf16),
            pltpu.VMEM(value_turned.shape, bf16),
            pltpu.VMEM(key_wide.shape, bf16),
            pltpu.VMEM(context.shape, bf16),
            pltpu.VMEM(query.shape, bf16),
            pltpu.VMEM(tokens.shape, bf16),
            pltpu.VMEM(project_weight.shape, bf16),
            pltpu.VMEM((4, heads, BACK_ROWS, keys), bf16),
            pltpu.VMEM((2, BACK_ROWS, width), f32),
            pltpu.VMEM((heads, HEAD, keys), f32),
            pltpu.VMEM((heads, HEAD, keys), f32),
            pltpu.VMEM((3, keys, width), bf16),
            pltpu.VMEM((row_count, width), bf16),
            pltpu.VMEM((row_count, width), bf16),
            pltpu.VMEM((2, half_rows, width), f32),
            pltpu.VMEM((4, BACK_ROWS, keys), jnp.int16),
            pltpu.VMEM((4, BACK_ROWS, keys), jnp.int16),
            pltpu.VMEM((high_rows * STRIP, low_lanes), f32),
            pltpu.VMEM((CHUNKS, CHUNK, CHUNK), bf16),
            pltpu.VMEM((away, CHUNK, CHUNK), bf16),
            pltpu.VMEM((CHUNKS, PARTS[0], CHUNK), bf16),
            pltpu.VMEM((away, PARTS[0], CHUNK), bf16),
            pltpu.VMEM((CHUNKS, PARTS[1], CHUNK), bf16),
            pltpu.VMEM((away, PARTS[1], CHUNK), bf16),
            pltpu.VMEM((away, PARTS[1], CHUNK), bf16),
            pltpu.VMEM((CHUNKS, PARTS[2], CHUNK), bf16),
            pltpu.VMEM((CHUNKS, PARTS[3], CHUNK), bf16),
            pltpu.VMEM((6, *small.shape), f32),
            pltpu.VMEM((5, *small.shape), f32),
            pltpu.VMEM((5, *table_shape), f32),
            pltpu.VMEM((4, *table_shape), f32),
            dma((9,)),
            dma((2, 2)),
            dma((4, 3)),
            dma((CHUNKS, 2)),
            dma((CHUNKS,)),
            dma((5,)),
            dma((CHUNKS, 11)),
            dma((CHUNKS, 11)),
            dma((3,)),
            dma((3,)),
            dma((5,)),
            dma((5,)),
            dma((4,)),
            dma((4,)),
        ],
        compiler_params=pltpu.CompilerParams(
            vmem_limit_bytes=FINISH_VMEM, collective_id=0, has_side_effects=True
        ),
        name="finish",
    )(
        exps,
        inverse,
        plane,
        down,
        context,
        query,
        tokens,
        grad,
        layer,
        value_turned,
        key_wide,
        project_weight,
        output_weight,
        *expand,
        *reduce,
        small,
    )
    return total, layer_full, input_full, table_sum, small_sum


UNPACK_ROWS = 96


def unpack_kernel(
    total_ref,
    layer_in_ref,
    input_in_ref,
    sum_ref,
    small_ref,
    layer_ref,
    input_ref,
    project_ref,
    output_ref,
    expand_ref,
    reduce_ref,
    line_ref,
    across_ref,
    down_ref,
    bias_ref,
    second_gain_ref,
    second_shift_ref,
    reduce_bias_ref,
    first_gain_ref,
    first_shift_ref,
    output_bias_ref,
    expand_bias_ref,
    *,
    high_counts,
):
    step = pl.program_id(0)
    layer_ref[...] = layer_in_ref[...]
    input_ref[...] = input_in_ref[...].reshape(input_ref.shape)
    values = total_ref[...].astype(f32)

    @pl.when(step < 3)
    def _():
        project_ref[0] = values.T

    @pl.when(step == 3)
    def _():
        output_ref[...] = values

    @pl.when((step >= 4) & (step < 8))
    def _():
        expand_ref[...] = values

    @pl.when(step >= 8)
    def _():
        reduce_ref[...] = values

    @pl.when(step == 0)
    def _():
        lanes = sum_ref.shape[1]
        row = lax.broadcasted_iota(jnp.int32, (lanes, LANES), 0) // STRIP
        same = row == lax.broadcasted_iota(jnp.int32, (lanes, LANES), 1)
        folded = jnp.dot(
            sum_ref[...],
            jnp.where(same, 1.0, 0.0),
            precision=lax.Precision.HIGHEST,
            preferred_element_type=f32,
        )
        heads = line_ref.shape[0]
        start = 0
        for ref, count in zip((line_ref, across_ref, down_ref), high_counts):
            parts = []
            for _ in range(count):
                parts.append(folded[start : start + heads, : lanes // STRIP])
                start += heads
            ref[...] = jnp.concatenate(parts, axis=1)
        half = bias_ref.shape[1] - lanes
        middle = sum_ref[start + 1 : start + 2, :]
        bias_ref[0:1, :] = jnp.concatenate([sum_ref[start : start + 1, :], middle[:, :half]], axis=1)
        bias_ref[1:2, :] = jnp.concatenate([middle[:, half:], sum_ref[start + 2 : start + 3, :]], axis=1)
        lead = lax.axis_index("mp") == 0
        for n, ref in enumerate(
            (
                second_gain_ref,
                second_shift_ref,
                reduce_bias_ref,
                first_gain_ref,
                first_shift_ref,
                output_bias_ref,
            )
        ):
            row = small_ref[n : n + 1, :]
            if ref.shape[0] < row.shape[1]:
                cut = ref.shape[0]
                row = jnp.where(lead, row[:, :cut], row[:, cut:])
            ref[...] = row.reshape(ref.shape)
        pieces = expand_bias_ref.shape[0] // small_ref.shape[1]
        width = small_ref.shape[1]
        for k in range(pieces):
            even = small_ref[8 + k : 9 + k, :]
            odd = small_ref[8 + pieces + k : 9 + pieces + k, :]
            expand_bias_ref[k * width : (k + 1) * width] = jnp.where(lead, even, odd).reshape(width)


def unpack(total, layer, inputs, sums, small, length, heads, counts):
    width = inputs.shape[1]
    depth = layer.shape[1]
    high_counts = (counts[0] // 16, counts[1] // 16, counts[1] // 16)
    half = CHUNK // 2
    steps = CHUNKS * 2

    def whole(shape):
        return pl.BlockSpec(shape, lambda i: (0,) * len(shape))

    def rows(columns):
        return pl.BlockSpec((UNPACK_ROWS, columns), lambda i: (i, 0))

    shapes = [
        ((length, depth), bf16),
        ((length, 1, width), f32),
        ((3, depth, width), f32),
        ((width, depth), f32),
        ((CHUNK, 2 * CHUNK), f32),
        ((2 * CHUNK, CHUNK), f32),
        ((heads, counts[0]), f32),
        ((heads, counts[1]), f32),
        ((heads, counts[1]), f32),
        ((2, width), f32),
        ((depth,), f32),
        ((depth,), f32),
        ((depth,), f32),
        ((width,), f32),
        ((width,), f32),
        ((depth,), f32),
        ((2 * CHUNK,), f32),
    ]
    return pl.pallas_call(
        partial(unpack_kernel, high_counts=high_counts),
        grid=(steps,),
        in_specs=[
            pl.BlockSpec((half, CHUNK), lambda i: (i, 0)),
            rows(depth),
            rows(width),
            whole(sums.shape),
            whole(small.shape),
        ],
        out_specs=[
            rows(depth),
            pl.BlockSpec((UNPACK_ROWS, 1, width), lambda i: (i, 0, 0)),
            pl.BlockSpec((1, depth, width), lambda i: (jnp.clip(i, 0, 2), 0, 0)),
            whole((width, depth)),
            pl.BlockSpec(
                (half, CHUNK),
                lambda i: (lax.rem(jnp.clip(i - 4, 0, 3), 2), jnp.clip(i - 4, 0, 3) // 2),
            ),
            pl.BlockSpec((half, CHUNK), lambda i: (jnp.clip(i - 8, 0, 3), 0)),
            *(whole(shape) for shape, _ in shapes[6:]),
        ],
        out_shape=[jax.ShapeDtypeStruct(shape, kind) for shape, kind in shapes],
        compiler_params=pltpu.CompilerParams(vmem_limit_bytes=vmem_limit),
        name="unpack",
    )(total, layer, inputs, sums, small)


def feed_kernel(
    context_ref,
    context_away_ref,
    token_ref,
    cotangent_ref,
    valid_ref,
    output_ref,
    output_away_ref,
    expand_ref,
    expand_away_ref,
    reduce_ref,
    reduce_away_ref,
    expand_bias_ref,
    expand_bias_away_ref,
    output_bias_ref,
    first_gain_ref,
    first_shift_ref,
    reduce_bias_ref,
    second_gain_ref,
    second_shift_ref,
    layer_ref,
    grad_ref,
    expand_grad_ref,
    expand_grad_away_ref,
    reduce_grad_ref,
    reduce_grad_away_ref,
    small_ref,
    input_buf,
    norm_buf,
    hat_buf,
    inverse_buf,
    total_buf,
    reduced_buf,
    active_buf,
    slope_buf,
    before_buf,
    vector_ref,
    bias_buf,
    *,
    pieces,
    tiles,
):
    rows, width = token_ref.shape
    step = pl.program_id(0)
    piece = step % (2 * pieces)
    strip_rows = FEED_STRIP
    strips = rows // strip_rows

    def vector(n):
        return vector_ref[n : n + 1, :]

    def for_strips(body, sums):
        def run(n, carry):
            at = pl.ds(pl.multiple_of(n * strip_rows, STRIP), strip_rows)
            return tuple(
                old + jnp.sum(new.reshape(strip_rows // 8, 8, width), axis=0)
                for old, new in zip(carry, body(at))
            )

        start = tuple(jnp.zeros((8, width), f32) for _ in range(sums))
        done = lax.fori_loop(0, strips, run, start)
        return [jnp.sum(part, axis=0, keepdims=True) for part in done]

    def mean(values):
        return jnp.sum(values, axis=-1, keepdims=True) * (1.0 / width)

    @pl.when(step == 0)
    def _():
        small_ref[...] = jnp.zeros_like(small_ref)
        for n, ref in enumerate(
            (
                output_bias_ref,
                first_gain_ref,
                first_shift_ref,
                reduce_bias_ref,
                second_gain_ref,
                second_shift_ref,
            )
        ):
            vector_ref[n : n + 1, :] = ref[...].astype(f32).reshape(1, width)
        bias = expand_bias_ref[...].astype(f32).reshape(1, -1)
        for k in range(pieces):
            cols = slice(k * expand_ref.shape[1], (k + 1) * expand_ref.shape[1])
            bias_buf[k : k + 1, :] = bias[:, cols]
            bias_buf[pieces + k : pieces + k + 1, :] = expand_bias_away_ref[0:1, cols]
        total_buf[...] = dot_f32(context_ref[...], output_ref[...]) + dot_f32(
            context_away_ref[...], output_away_ref[...]
        )

        def body(at):
            values = token_ref[at, :].astype(f32) + (total_buf[at, :] + vector(0))
            centered = values - mean(values)
            inverse = lax.rsqrt(mean(centered * centered) + norm_epsilon)
            hat = centered * inverse
            norm = hat * vector(1) + vector(2)
            hat_buf[at, :] = hat
            inverse_buf[at, :] = jnp.broadcast_to(inverse, (strip_rows, LANES))
            norm_buf[at, :] = norm
            input_buf[at, :] = norm.astype(bf16)
            total_buf[at, :] = norm + vector(3)
            return ()

        for_strips(body, 0)

    def forward(expand, reduce):
        for start, size in tiles:
            at = slice(start, start + size)
            before = dot_f32(input_buf[at, :], expand[...]) + bias_buf[pl.ds(piece, 1), :]
            phi = 0.5 * lax.erf(before * 0.7071067811865476) + 0.5
            slope_buf[piece, at, :] = phi + before * (
                0.3989422804014327 * jnp.exp(-0.5 * (before * before))
            )
            active = (before * phi).astype(bf16)
            active_buf[piece, at, :] = active
            total_buf[at, :] += dot_f32(active, reduce[...])

    pl.when(step < pieces)(lambda: forward(expand_ref, reduce_ref))
    pl.when((step >= pieces) & (step < 2 * pieces))(
        lambda: forward(expand_away_ref, reduce_away_ref)
    )

    @pl.when(step == 2 * pieces)
    def _():
        def body(at):
            values = total_buf[at, :]
            valid = valid_ref[at, 0:1]
            centered = values - mean(values)
            inverse = lax.rsqrt(mean(centered * centered) + norm_epsilon)
            hat = centered * inverse
            layer_ref[at, :] = (valid * (hat * vector(4) + vector(5))).astype(bf16)
            grad_out = jnp.where(valid > 0, cotangent_ref[at, :].astype(f32), 0.0)
            grad_hat = grad_out * vector(4)
            mixed = inverse * (grad_hat - mean(grad_hat) - hat * mean(grad_hat * hat))
            low = mixed.astype(bf16)
            reduced_buf[at, :] = low
            total_buf[at, :] = mixed
            return grad_out * hat, grad_out, low.astype(f32)

        for n, part in enumerate(for_strips(body, 3)):
            small_ref[n : n + 1, :] = part

    def backward(expand, reduce):
        sums = None
        for start, size in tiles:
            at = slice(start, start + size)
            grad_active = lax.dot_general(
                reduced_buf[at, :], reduce[...], (((1,), (1,)), ((), ())), preferred_element_type=f32
            )
            before = (grad_active * slope_buf[piece, at, :]).astype(bf16)
            before_buf[piece, at, :] = before
            part = jnp.sum(before.astype(f32), axis=0, keepdims=True)
            sums = part if sums is None else sums + part
            total_buf[at, :] += lax.dot_general(
                before, expand[...], (((1,), (1,)), ((), ())), preferred_element_type=f32
            )
        mp_index = lax.axis_index("mp")
        side = jnp.where(piece < pieces, mp_index, 1 - mp_index)
        small_ref[pl.ds(8 + side * pieces + lax.rem(piece, pieces), 1), :] = sums

    pl.when((step >= 2 * pieces) & (step < 3 * pieces))(lambda: backward(expand_ref, reduce_ref))
    pl.when((step >= 3 * pieces) & (step < 4 * pieces))(
        lambda: backward(expand_away_ref, reduce_away_ref)
    )

    @pl.when(step == 4 * pieces)
    def _():
        def body(at):
            grad_first = total_buf[at, :]
            hat = hat_buf[at, :]
            grad_hat = grad_first * vector(1)
            inverse = inverse_buf[at, 0:1]
            inner = inverse * (grad_hat - mean(grad_hat) - hat * mean(grad_hat * hat))
            low = inner.astype(bf16)
            grad_ref[at, :] = low
            return grad_first * hat, grad_first, low.astype(f32)

        for n, part in enumerate(for_strips(body, 3)):
            small_ref[n + 3 : n + 4, :] = part

    def weights(expand_grad, reduce_grad):
        reduce_grad[...] = lax.dot_general(
            active_buf[piece], reduced_buf[...], (((0,), (0,)), ((), ())), preferred_element_type=f32
        ).astype(bf16)
        expand_grad[...] = lax.dot_general(
            input_buf[...], before_buf[piece], (((0,), (0,)), ((), ())), preferred_element_type=f32
        ).astype(bf16)

    pl.when((step >= 4 * pieces) & (step < 5 * pieces))(
        lambda: weights(expand_grad_ref, reduce_grad_ref)
    )
    pl.when(step >= 5 * pieces)(lambda: weights(expand_grad_away_ref, reduce_grad_away_ref))


def feed(
    context,
    context_away,
    tokens,
    cotangent,
    valid,
    output,
    output_away,
    expand,
    expand_away,
    reduce,
    reduce_away,
    expand_bias,
    expand_bias_away,
    vectors,
):
    rows, width = context_away.shape[0], tokens.shape[1]
    hidden = expand.shape[1]
    size = FEED_PIECE
    pieces = hidden // size
    split = round_up(rows // 2, STRIP)
    tiles = ((0, split), (split, rows - split))

    def once(array):
        zeros = (0,) * array.ndim
        return pl.BlockSpec(array.shape, lambda i: zeros, pipeline_mode=pl.Buffered(1))

    def mine(array):
        return pl.BlockSpec(
            (rows, array.shape[1]),
            lambda i: (lax.axis_index("mp"), 0),
            pipeline_mode=pl.Buffered(1),
        )

    def place(first, i):
        at = lax.rem(i, 2 * pieces) - first
        at = jnp.clip(at, 0, pieces - 1)
        return jnp.where(i < 4 * pieces, at, pieces - 1)

    def grad_place(first, i):
        return jnp.clip(i - 4 * pieces - first, 0, pieces - 1)

    wide = lambda first: pl.BlockSpec((width, size), lambda i: (0, place(first, i)))
    tall = lambda first: pl.BlockSpec((size, width), lambda i: (place(first, i), 0))
    wide_grad = lambda first: pl.BlockSpec((width, size), lambda i: (0, grad_place(first, i)))
    tall_grad = lambda first: pl.BlockSpec((size, width), lambda i: (grad_place(first, i), 0))
    whole = lambda shape: pl.BlockSpec(
        shape, lambda i: (0,) * len(shape), pipeline_mode=pl.Buffered(1)
    )
    full = jax.ShapeDtypeStruct((rows, width), bf16)
    return pl.pallas_call(
        partial(feed_kernel, pieces=pieces, tiles=tiles),
        grid=(6 * pieces,),
        in_specs=[
            mine(context),
            once(context_away),
            mine(tokens),
            mine(cotangent),
            mine(valid),
            once(output),
            once(output_away),
            wide(0),
            wide(pieces),
            tall(0),
            tall(pieces),
            once(expand_bias),
            once(expand_bias_away),
            *(once(vector) for vector in vectors),
        ],
        out_specs=[
            whole((rows, width)),
            whole((rows, width)),
            wide_grad(0),
            wide_grad(pieces),
            tall_grad(0),
            tall_grad(pieces),
            whole((16, width)),
        ],
        out_shape=[
            full,
            full,
            jax.ShapeDtypeStruct((width, hidden), bf16),
            jax.ShapeDtypeStruct((width, hidden), bf16),
            jax.ShapeDtypeStruct((hidden, width), bf16),
            jax.ShapeDtypeStruct((hidden, width), bf16),
            jax.ShapeDtypeStruct((16, width), f32),
        ],
        scratch_shapes=[
            pltpu.VMEM((rows, width), bf16),
            pltpu.VMEM((rows, width), f32),
            pltpu.VMEM((rows, width), f32),
            pltpu.VMEM((rows, LANES), f32),
            pltpu.VMEM((rows, width), f32),
            pltpu.VMEM((rows, width), bf16),
            pltpu.VMEM((2 * pieces, rows, size), bf16),
            pltpu.VMEM((2 * pieces, rows, size), f32),
            pltpu.VMEM((2 * pieces, rows, size), bf16),
            pltpu.VMEM((8, width), f32),
            pltpu.VMEM((2 * pieces, size), f32),
        ],
        compiler_params=pltpu.CompilerParams(vmem_limit_bytes=vmem_limit),
        name="feed",
    )(
        context,
        context_away,
        tokens,
        cotangent,
        valid,
        output,
        output_away,
        expand,
        expand_away,
        reduce,
        reduce_away,
        expand_bias,
        expand_bias_away,
        *vectors,
    )


def swap(array):
    return lax.ppermute(array, "mp", [(0, 1), (1, 0)])


def partner(array, count, bit):
    return lax.ppermute(array, "dp", [(i, i ^ bit) for i in range(count)])


def sum_rows_over_dp(array, count):
    place = lax.axis_index("dp")
    bits = []
    bit = 1
    while bit < count:
        mine = (place // bit) % 2
        halves = array.reshape((2, array.shape[0] // 2) + array.shape[1:])
        sent = lax.dynamic_index_in_dim(halves, 1 - mine, 0, keepdims=False)
        kept = lax.dynamic_index_in_dim(halves, mine, 0, keepdims=False)
        array = kept + partner(sent, count, bit)
        bits.append(bit)
        bit *= 2
    for bit in reversed(bits):
        lead = (place // bit) % 2 == 0
        other = partner(array, count, bit)
        array = jnp.concatenate(
            [jnp.where(lead, array, other), jnp.where(lead, other, array)], axis=0
        )
    return array


def sum_small(arrays, count, over_mp):
    sizes = [a.size for a in arrays]
    total = sum(sizes)
    flat = jnp.concatenate([a.reshape(-1) for a in arrays])
    flat = jnp.pad(flat, (0, round_up(total, 1024) - total)).reshape(-1, LANES)
    if over_mp:
        flat = flat + swap(flat)
    bit = 1
    while bit < count:
        flat = flat + partner(flat, count, bit)
        bit *= 2
    flat = flat.reshape(-1)
    outs = []
    start = 0
    for array, size in zip(arrays, sizes):
        outs.append(flat[start : start + size].reshape(array.shape))
        start += size
    return outs


def per_device(
    dp_count,
    tokens,
    cotangent,
    long_flag,
    token_mask,
    bucket_line,
    bucket_across,
    bucket_down,
    project_weight,
    project_bias,
    table_line,
    table_across,
    table_down,
    output_weight,
    output_bias,
    first_gain,
    first_shift,
    expand_weight,
    expand_bias,
    reduce_weight,
    reduce_bias,
    second_gain,
    second_shift,
):
    length = tokens.shape[1]
    width = project_weight.shape[2]
    heads = table_line.shape[1]
    counts = (table_line.shape[0], table_across.shape[0])
    rows = round_up(length, BLOCK_ROWS)
    half_rows = rows // 2
    keys = round_up(length, 3 * LANES)
    mp_index = lax.axis_index("mp")
    lead = mp_index == 0

    def own_rows(array):
        return lax.dynamic_slice_in_dim(array, mp_index * half_rows, half_rows, 0)

    def in_order(mine, other):
        return jnp.where(lead, mine, other), jnp.where(lead, other, mine)


    (
        query,
        key_wide,
        key_turned,
        value_ones,
        value_turned,
        padded,
        plane,
        down,
        valid_rows,
        expand_quarter,
    ) = prepare(
        tokens[0],
        project_weight,
        project_bias,
        (bucket_line, bucket_across, bucket_down),
        long_flag,
        token_mask,
        expand_weight,
        rows,
        keys,
        counts[0],
    )
    (
        exps,
        context,
        inverse,
        context_away,
        expand_away,
        output_away,
        reduce_away,
        expand_bias_away,
    ) = attend(
        query,
        key_turned,
        value_ones,
        plane,
        down,
        (table_line.T, table_across.T, table_down.T),
        expand_bias,
        expand_quarter,
        output_weight,
        reduce_weight,
    )

    (
        layer_mine,
        grad_mine,
        expand_own,
        expand_sent,
        reduce_own,
        reduce_sent,
        small,
    ) = feed(
        context,
        context_away,
        padded,
        cotangent[0],
        valid_rows,
        output_weight,
        output_away,
        expand_weight,
        expand_away,
        reduce_weight,
        reduce_away,
        expand_bias,
        expand_bias_away,
        (output_bias, first_gain, first_shift, reduce_bias, second_gain, second_shift),
    )
    if dp_count == 16 and expand_own.shape == (CHUNK, 2 * CHUNK):
        total, layer_full, input_full, sums, small = finish(
            exps,
            inverse,
            plane,
            down,
            context,
            query,
            padded,
            grad_mine,
            layer_mine,
            value_turned,
            key_wide,
            project_weight,
            output_weight,
            (expand_own, expand_sent),
            (reduce_own, reduce_sent),
            small,
            counts,
        )
        (
            layer_out,
            input_grad,
            project_weight_grad,
            output_weight_grad,
            expand_weight_grad,
            reduce_weight_grad,
            line_grad,
            across_grad,
            down_grad,
            project_bias_grad,
            second_gain_grad,
            second_shift_grad,
            reduce_bias_grad,
            first_gain_grad,
            first_shift_grad,
            output_bias_grad,
            expand_bias_grad,
        ) = unpack(total, layer_full, input_full, sums, small, length, heads, counts)
        layer_out = layer_out[None]
        input_grad = input_grad.reshape(1, length, width)
        table_grads = (line_grad.T, across_grad.T, down_grad.T)
    else:
        layer_out = jnp.concatenate(in_order(layer_mine, swap(layer_mine)))[None, :length]
        grad_attended = jnp.concatenate(in_order(grad_mine, swap(grad_mine)))
        output_weight_grad = jnp.einsum(
            "le,lf->ef", context, grad_attended, preferred_element_type=f32
        ).astype(bf16)
        grad_context = jnp.einsum(
            "lf,ef->le", grad_attended, output_weight, preferred_element_type=f32
        )
        grad_scaled = (grad_context * inverse).astype(bf16)
        grad_scores, grad_query, grad_key, grad_value = attend_back(
            exps, grad_scaled, context, query, value_turned, key_wide
        )
        grad_key = grad_key.reshape(width, keys)[:, :rows].T.astype(bf16)
        grad_value = grad_value.reshape(width, keys)[:, :rows].T.astype(bf16)
        triple = jnp.stack([grad_query, grad_key, grad_value])
        project_weight_grad = jnp.einsum(
            "ld,kle->kde", padded[:rows], triple, preferred_element_type=f32
        ).astype(bf16)
        project_bias_grad = jnp.stack(
            [jnp.sum(grad_query, axis=0, dtype=f32), jnp.sum(grad_value, axis=0, dtype=f32)]
        )
        input_part = jnp.einsum("kle,kde->ld", triple, project_weight, preferred_element_type=f32)
        input_part = lax.dynamic_update_slice_in_dim(
            input_part,
            own_rows(input_part) + grad_mine.astype(f32),
            mp_index * half_rows,
            0,
        )
        sent = jnp.where(lead, input_part[:, width:], input_part[:, :width]).astype(bf16)
        own = jnp.where(lead, input_part[:, :width], input_part[:, width:])
        input_grad = (own + swap(sent).astype(f32))[None, :length]
        table_grads = table_sums(grad_scores, plane, down, counts)
        reduce_weight_grad = sum_rows_over_dp(reduce_own + swap(reduce_sent), dp_count)
        expand_weight_grad = sum_rows_over_dp(expand_own + swap(expand_sent), dp_count)
        output_weight_grad = sum_rows_over_dp(output_weight_grad, dp_count)
        project_weight_grad = sum_rows_over_dp(
            project_weight_grad.reshape(-1, width), dp_count
        ).reshape(project_weight.shape)
        (small,) = sum_small([small], dp_count, True)
        bias_rows = expand_bias.size // small.shape[1]
        bias_rows = lax.dynamic_slice_in_dim(small, 8 + mp_index * bias_rows, bias_rows, 0)
        expand_bias_grad = bias_rows.reshape(-1)
        (
            second_gain_grad,
            second_shift_grad,
            reduce_bias_grad,
            first_gain_grad,
            first_shift_grad,
            output_bias_grad,
        ) = (small[n] for n in range(6))
        first_gain_grad = lax.dynamic_slice_in_dim(first_gain_grad, mp_index * width, width, 0)
        first_shift_grad = lax.dynamic_slice_in_dim(first_shift_grad, mp_index * width, width, 0)
        table_grads, project_bias_grad = sum_small(
            [table_grads, project_bias_grad], dp_count, False
        )
        cuts = (counts[0], counts[0] + counts[1])
        table_grads = (
            table_grads[: cuts[0]],
            table_grads[cuts[0] : cuts[1]],
            table_grads[cuts[1] :],
        )
    return (
        layer_out,
        input_grad,
        project_weight_grad.astype(f32),
        project_bias_grad,
        *table_grads,
        output_weight_grad.astype(f32),
        output_bias_grad,
        first_gain_grad,
        first_shift_grad,
        expand_weight_grad.astype(f32),
        expand_bias_grad,
        reduce_weight_grad.astype(f32),
        reduce_bias_grad,
        second_gain_grad,
        second_shift_grad,
    )


def solution(mesh):
    placed = (
        P("dp", None, None),
        P("dp", None, None),
        P("dp"),
        P("dp", None),
        P("dp", None, None),
        P("dp", None, None),
        P("dp", None, None),
        P(None, None, "mp"),
        P(None, "mp"),
        P(None, "mp"),
        P(None, "mp"),
        P(None, "mp"),
        P("mp", None),
        P(),
        P(),
        P(),
        P(None, "mp"),
        P("mp"),
        P("mp", None),
        P(),
        P(),
        P(),
    )
    return jax.shard_map(
        partial(per_device, mesh.shape["dp"]),
        mesh=mesh,
        in_specs=placed,
        out_specs=(
            P("dp", None, None),
            P("dp", None, "mp"),
            P(None, None, "mp"),
            P(None, "mp"),
            P(None, "mp"),
            P(None, "mp"),
            P(None, "mp"),
            P("mp", None),
            P(),
            P("mp"),
            P("mp"),
            P(None, "mp"),
            P("mp"),
            P("mp", None),
            P(),
            P(),
            P(),
        ),
        check_vma=False,
    )
```

profile of v0, /device:TPU:0, one launch (start us, length us, event | category | flops | bytes accessed | tf_op | source)
XLA Modules:
  0.0 257.7 jit_solution(6306039161281311276)
XLA Ops:
  1.3 24.6 %prepare.1 = (bf16[1152,384]{1,0:T(8,128)(2,1)}, bf16[6,1152,128]{2,1,0:T(8,128)(2,1)}, bf16[6,128,1152]{2,1,0:T(8,128)(2,1)}, bf16[6,1152,128]{2,1,0:T(8,128)(2...) custom-call(bf16[1089,768]{1,0:T(8,128)(2,1)} %bitcast.16, ...), custom_call_target="tpu_custom_call" | custom-call | tf_op jit(solution)/shard_map/prepare/pallas_call | solution.py:168
  25.9 45.6 %attend.1 = (bf16[6,1120,1152]{2,1,0:T(8,128)(2,1)}, bf16[1120,384]{1,0:T(8,128)(2,1)}, f32[1120,384]{1,0:T(8,128)}, bf16[560,384]{1,0:T(8,128)(2,1)}, bf16[768,...) custom-call(bf16[1152,384]{1,0:T(8,128)(2,1)} %get-tuple-element.64.query_ref, ...), custom_call_target="tpu_custom_call" | custom-call | tf_op jit(solution)/shard_map/attend/pallas_call | solution.py:452
  71.6 37.6 %feed.1 = (bf16[560,768]{1,0:T(8,128)(2,1)}, bf16[560,768]{1,0:T(8,128)(2,1)}, bf16[768,1536]{1,0:T(8,128)(2,1)}, bf16[768,1536]{1,0:T(8,128)(2,1)}, bf16[1536,7...) custom-call(bf16[1120,384]{1,0:T(8,128)(2,1)} %get-tuple-element.72.context_ref, ...), custom_call_target="tpu_custom_call" | custom-call | tf_op jit(solution)/shard_map/feed/pallas_call | solution.py:1842
  109.2 133.5 %finish.1 = (bf16[4608,768]{1,0:T(8,128)(2,1)}, bf16[1120,768]{1,0:T(8,128)(2,1)}, f32[1120,384]{1,0:T(8,128)}, f32[16,768]{1,0:T(8,128)}, f32[64,256]{1,0:T(8,128)}, /*index=5*/bf16[6,1120,1152]{2,1,0:T(8,128)(2,1)}) custom-call(bf16[6,1120,1152]{2,1,0:T(8,128)(2,1)} %get-tuple-element.70.exp_ref, f32[1120,384]{1,0:T(8,128)} %get-tuple-element.71.inverse_ref, ...), custom_call_target="tpu_custom_call" | custom-call | tf_op jit(solution)/shard_map/finish/pallas_call | solution.py:1357
  242.6 14.9 %unpack.1 = (bf16[1089,768]{1,0:T(8,128)(2,1)}, f32[1089,1,384]{2,1,0:T(1,128)}, f32[3,768,384]{2,1,0:T(8,128)}, f32[384,768]{1,0:T(8,128)}, f32[768,1536]{1,0:T...) custom-call(bf16[4608,768]{1,0:T(8,128)(2,1)} %get-tuple-element.89., ...), custom_call_target="tpu_custom_call" | custom-call | tf_op jit(solution)/shard_map/unpack/pallas_call | solution.py:1571
where the time goes:
time: 258 us
  Pallas kernels  256 us (99%)
    pallas_call x1, Pallas kernels, finish(): pl.pallas_call(partial(finish_kernel, high_counts=high_counts), in_specs=...  133 us
    pallas_call x1, Pallas kernels, attend(): pl.pallas_call(attend_kernel, grid=(2,), in_specs=[row_spec, whole_spec(k...  45.6 us
    pallas_call x1, Pallas kernels, feed(): pl.pallas_call(partial(feed_kernel, pieces=pieces, tiles=tiles), grid=(6...  37.6 us
    pallas_call x1, Pallas kernels, prepare(): pl.pallas_call(partial(prepare_kernel, length=length, line_count=line_cou...  24.6 us
    pallas_call x1, Pallas kernels, unpack(): pl.pallas_call(partial(unpack_kernel, high_counts=high_counts), grid=(ste...  14.9 us

commit v1 on v0

--- a/solution.py
+++ b/solution.py
@@ -112,7 +112,6 @@
         row_ref[...] = jnp.zeros_like(row_ref)
         row_ref[0:1, :length] = jnp.where((mask_ref[...] > 0) & (position < limit), 1.0, 0.0)
 
-    pl.when(step == pl.num_programs(0) - 1)(fetch.wait)
     rows = token_ref.shape[0]
     keys = plane_ref.shape[1]
     place = pl.program_id(0) * rows + lax.broadcasted_iota(jnp.int32, token_ref.shape, 0)
@@ -149,6 +148,7 @@
             value_ref[h] = jnp.where(lane_own, value_pair, 1.0).astype(bf16)
             key_turned_ref[h] = jnp.where(row_own, key_turned, 0.0).astype(bf16)
             value_turned_ref[h] = jnp.where(row_own, value_turned, 0.0).astype(bf16)
+    pl.when(step == pl.num_programs(0) - 1)(fetch.wait)
 
 
 def prepare(tokens, weight, bias, buckets, flag, token_mask, expand, row_count, keys, line_count):
@@ -236,7 +236,7 @@
     expand_quarter_ref,
     output_ref,
     reduce_ref,
-    exp_ref,
+    exp_out_ref,
     context_ref,
     inverse_ref,
     context_away_ref,
@@ -245,15 +245,19 @@
     reduce_away_ref,
     bias_away_ref,
     score_ref,
+    exp_ref,
     send_ref,
     table_ref,
     bias_ref,
+    exp_sem,
     local_sem,
     send_sem,
     recv_sem,
 ):
-    heads, rows, keys = exp_ref.shape
+    _, heads, rows, keys = exp_ref.shape
     step = pl.program_id(0)
+    turn_rows = ATTEND_STRIPS * STRIP
+    turns = rows // turn_rows
     place = lax.axis_index("dp")
     across_mp = {"mp": 1 - lax.axis_index("mp")}
     across = {bit: {"dp": place + bit * (1 - 2 * ((place // bit) % 2))} for bit in (1, 2)}
@@ -297,6 +301,14 @@
     def arrival(n, stage):
         region = rows_of(n, (other_chip, other_core, third)[stage])
         return remote(region, region, 3 + 3 * stage + n, across_mp)
+
+    def exp_copy(which, turn):
+        half = lax.rem(which + 1 - lax.axis_index("mp"), 2)
+        here = pl.ds(pl.multiple_of(turn * turn_rows, STRIP), turn_rows)
+        there = pl.ds(pl.multiple_of(half * rows + turn * turn_rows, STRIP), turn_rows)
+        return pltpu.make_async_copy(
+            exp_ref.at[which, :, here, :], exp_out_ref.at[:, there, :], exp_sem.at[which, turn]
+        )
 
     keep = pltpu.make_async_copy(expand_quarter_ref, rows_of(0, quarter), local_sem)
     context_swap = remote(send_ref, context_away_ref, 12, across_mp)
@@ -383,22 +395,23 @@
                 for piece in pieces:
                     event(*piece)
 
-        start = pl.multiple_of(n * ATTEND_STRIPS * STRIP, STRIP)
+        start = pl.multiple_of(n * turn_rows, STRIP)
         places = [pl.ds(start + k * STRIP, STRIP) for k in range(ATTEND_STRIPS)]
         scores = [scores_of(at) for at in places]
         exps = [exps_of(part) for part in scores]
         for at, part in zip(places, exps):
             for h in range(heads):
                 for c, cols in enumerate(lanes):
-                    exp_ref[h, at, cols] = part[h][c]
+                    exp_ref[step, h, at, cols] = part[h][c]
+        exp_copy(step, n).start()
         return carry
 
-    lax.fori_loop(0, rows // (ATTEND_STRIPS * STRIP), strips, 0)
+    lax.fori_loop(0, turns, strips, 0)
     first = lax.broadcasted_iota(jnp.int32, (rows, LANES), 1) < HEAD
     for p in range(heads // 2):
         cols = slice(p * LANES, (p + 1) * LANES)
-        even = dot_f32(exp_ref[2 * p], value_ref[2 * p])
-        odd = dot_f32(exp_ref[2 * p + 1], value_ref[2 * p + 1])
+        even = dot_f32(exp_ref[step, 2 * p], value_ref[2 * p])
+        odd = dot_f32(exp_ref[step, 2 * p + 1], value_ref[2 * p + 1])
         sums = jnp.where(first, pltpu.roll(even, HEAD, 1), pltpu.roll(odd, HEAD, 1))
         inverse = 1.0 / sums
         inverse_ref[:, cols] = inverse
@@ -414,6 +427,9 @@
     @pl.when(step == 1)
     def _():
         event(2, "passed")
+        for which in range(2):
+            for n in range(turns):
+                exp_copy(which, n).wait()
         keep.wait()
         context_swap.wait()
         bias_swap.wait()
@@ -465,7 +481,7 @@
             anywhere,
         ],
         out_specs=[
-            pl.BlockSpec((heads, half_rows, keys), lambda i: (0, half(i), 0)),
+            anywhere,
             row_spec,
             row_spec,
             anywhere,
@@ -486,9 +502,11 @@
         ],
         scratch_shapes=[
             pltpu.VMEM((heads, half_rows, keys), f32),
+            pltpu.VMEM((2, heads, half_rows, keys), bf16),
             pltpu.VMEM((half_rows, width), bf16),
             pltpu.VMEM((3 * heads, STRIP, LANES), bf16),
             pltpu.VMEM((8, expand_bias.size), f32),
+            pltpu.SemaphoreType.DMA((2, half_rows // (ATTEND_STRIPS * STRIP))),
             pltpu.SemaphoreType.DMA,
             pltpu.SemaphoreType.DMA((14,)),
             pltpu.SemaphoreType.DMA((14,)),
@@ -696,15 +714,15 @@
     ("b", 8, 1, 4), ("b", 9, 1, 5), ("b", 20, 2, 2), ("b", 22, 2, 3), ("p", 0, 3, 2), ("p", 2, 2, 4),
     ("p", 3, 2, 5), ("p", 3, 3, 3), ("p", 3, 0, 0), ("p", 3, 0, 1), ("t", 0, 4, 2), ("t", 1, 1, 0),
     ("t", 1, 1, 1), ("t", 2, 4, 3), ("t", 2, "small", 0), ("t", 3, 3, 4), ("t", 4, 5, 2),
-    ("t", 5, "send", 0), ("t", 6, 3, 5), ("t", 6, 2, 0), ("t", 6, 2, 1), ("t", 6, "small", 1),
-    ("t", 8, 5, 3), ("t", 9, 4, 4), ("t", 10, 4, 5), ("t", 11, 6, 2), ("t", 11, "small", 2),
-    ("t", 12, 3, 1), ("t", 12, 3, 0), ("t", 13, 6, 3), ("t", 15, 5, 4), ("t", 16, "layer", 0),
-    ("t", 16, "small", 3), ("t", 17, 5, 5), ("t", 17, 7, 3), ("t", 18, 7, 2), ("t", 18, "input", 0),
-    ("t", 19, 4, 1), ("t", 19, 4, 0), ("t", 20, "small", 4), ("t", 21, 6, 4), ("t", 22, 8, 2),
-    ("t", 23, 6, 5), ("t", 24, 9, 2), ("t", 25, "small", 5), ("t", 26, 8, 3), ("t", 27, 5, 1),
-    ("t", 27, 7, 5), ("t", 28, 9, 3), ("t", 29, 5, 0), ("t", 29, 7, 4), ("t", 31, 6, 1),
-    ("t", 33, 8, 5), ("e", 0, 9, 5), ("e", 0, 8, 4), ("e", 0, 6, 0), ("e", 0, 9, 4), ("e", 0, 7, 1),
-    ("e", 0, 8, 1), ("e", 0, 7, 0), ("e", 0, 8, 0),
+    ("t", 6, 3, 5), ("t", 6, 2, 0), ("t", 6, 2, 1), ("t", 6, "small", 1), ("t", 8, 5, 3),
+    ("t", 9, 4, 4), ("t", 10, 4, 5), ("t", 11, 6, 2), ("t", 11, "send", 0), ("t", 11, "small", 2),
+    ("t", 12, 3, 1), ("t", 12, 3, 0), ("t", 13, 6, 3), ("t", 15, 5, 4), ("t", 16, "small", 3),
+    ("t", 17, 5, 5), ("t", 17, 7, 3), ("t", 18, 7, 2), ("t", 19, 4, 1), ("t", 20, "small", 4),
+    ("t", 21, 4, 0), ("t", 23, 6, 4), ("t", 24, 8, 2), ("t", 24, "input", 0), ("t", 25, 6, 5),
+    ("t", 25, 9, 2), ("t", 25, "small", 5), ("t", 26, 8, 3), ("t", 26, "layer", 0), ("t", 27, 5, 1),
+    ("t", 28, 9, 3), ("t", 29, 5, 0), ("t", 29, 7, 5), ("t", 29, 7, 4), ("t", 31, 6, 1),
+    ("t", 33, 6, 0), ("e", 0, 8, 4), ("e", 0, 9, 4), ("e", 0, 8, 5), ("e", 0, 9, 5), ("e", 0, 7, 0),
+    ("e", 0, 8, 0), ("e", 0, 7, 1), ("e", 0, 8, 1),
 )
 
 
@@ -1439,7 +1457,7 @@
     return total, layer_full, input_full, table_sum, small_sum
 
 
-UNPACK_ROWS = 96
+UNPACK_ROWS = 192
 
 
 def unpack_kernel(
@@ -1473,19 +1491,25 @@
     input_ref[...] = input_in_ref[...].reshape(input_ref.shape)
     values = total_ref[...].astype(f32)
 
-    @pl.when(step < 3)
+    half = values.shape[0] // 2
+
+    @pl.when(step < 2)
     def _():
-        project_ref[0] = values.T
-
-    @pl.when(step == 3)
+        project_ref[0] = values[:half].T
+
+    @pl.when(step == 0)
     def _():
-        output_ref[...] = values
-
-    @pl.when((step >= 4) & (step < 8))
+        project_ref[1] = values[half:].T
+
+    @pl.when(step == 1)
+    def _():
+        output_ref[...] = values[half:]
+
+    @pl.when((step >= 2) & (step < 4))
     def _():
         expand_ref[...] = values
 
-    @pl.when(step >= 8)
+    @pl.when(step >= 4)
     def _():
         reduce_ref[...] = values
 
@@ -1540,8 +1564,6 @@
     width = inputs.shape[1]
     depth = layer.shape[1]
     high_counts = (counts[0] // 16, counts[1] // 16, counts[1] // 16)
-    half = CHUNK // 2
-    steps = CHUNKS * 2
 
     def whole(shape):
         return pl.BlockSpec(shape, lambda i: (0,) * len(shape))
@@ -1570,9 +1592,9 @@
     ]
     return pl.pallas_call(
         partial(unpack_kernel, high_counts=high_counts),
-        grid=(steps,),
+        grid=(CHUNKS,),
         in_specs=[
-            pl.BlockSpec((half, CHUNK), lambda i: (i, 0)),
+            pl.BlockSpec((CHUNK, CHUNK), lambda i: (i, 0)),
             rows(depth),
             rows(width),
             whole(sums.shape),
@@ -1581,13 +1603,10 @@
         out_specs=[
             rows(depth),
             pl.BlockSpec((UNPACK_ROWS, 1, width), lambda i: (i, 0, 0)),
-            pl.BlockSpec((1, depth, width), lambda i: (jnp.clip(i, 0, 2), 0, 0)),
+            pl.BlockSpec((2, depth, width), lambda i: (jnp.minimum(i, 1), 0, 0)),
             whole((width, depth)),
-            pl.BlockSpec(
-                (half, CHUNK),
-                lambda i: (lax.rem(jnp.clip(i - 4, 0, 3), 2), jnp.clip(i - 4, 0, 3) // 2),
-            ),
-            pl.BlockSpec((half, CHUNK), lambda i: (jnp.clip(i - 8, 0, 3), 0)),
+            pl.BlockSpec((CHUNK, CHUNK), lambda i: (0, jnp.clip(i - 2, 0, 1))),
+            pl.BlockSpec((CHUNK, CHUNK), lambda i: (jnp.clip(i - 4, 0, 1), 0)),
             *(whole(shape) for shape, _ in shapes[6:]),
         ],
         out_shape=[jax.ShapeDtypeStruct(shape, kind) for shape, kind in shapes],

time: 258 us -> 248 us (0.961)
  Pallas kernels: 256 us -> 246 us
    pallas_call x1, Pallas kernels: 133 us -> 130 us  [finish(): pl.pallas_call(partial(finish_kernel, high_counts=high_counts), in_specs=...]
where the time goes in v1:
time: 248 us
  Pallas kernels  246 us (99%)
    pallas_call x1, Pallas kernels, finish(): pl.pallas_call(partial(finish_kernel, high_counts=high_counts), in_specs=...  130 us
    pallas_call x1, Pallas kernels, attend(): pl.pallas_call(attend_kernel, grid=(2,), in_specs=[row_spec, whole_spec(k...  43.2 us
    pallas_call x1, Pallas kernels, feed(): pl.pallas_call(partial(feed_kernel, pieces=pieces, tiles=tiles), grid=(6...  37.6 us
    pallas_call x1, Pallas kernels, prepare(): pl.pallas_call(partial(prepare_kernel, length=length, line_count=line_cou...  22.3 us
    pallas_call x1, Pallas kernels, unpack(): pl.pallas_call(partial(unpack_kernel, high_counts=high_counts), grid=(CHU...  12.7 us

profile of v1, /device:TPU:0, one launch (start us, length us, event | category | flops | bytes accessed | tf_op | source)
XLA Modules:
  0.0 247.7 jit_solution(2385224192031822616)
XLA Ops:
  1.3 22.3 %prepare.1 = (bf16[1152,384]{1,0:T(8,128)(2,1)}, bf16[6,1152,128]{2,1,0:T(8,128)(2,1)}, bf16[6,128,1152]{2,1,0:T(8,128)(2,1)}, bf16[6,1152,128]{2,1,0:T(8,128)(2...) custom-call(bf16[1089,768]{1,0:T(8,128)(2,1)} %bitcast.16, ...), custom_call_target="tpu_custom_call" | custom-call | tf_op jit(solution)/shard_map/prepare/pallas_call | solution.py:168
  23.6 43.2 %attend.1 = (bf16[6,1120,1152]{2,1,0:T(8,128)(2,1)}, bf16[1120,384]{1,0:T(8,128)(2,1)}, f32[1120,384]{1,0:T(8,128)}, bf16[560,384]{1,0:T(8,128)(2,1)}, bf16[768,...) custom-call(bf16[1152,384]{1,0:T(8,128)(2,1)} %get-tuple-element.64.query_ref, ...), custom_call_target="tpu_custom_call" | custom-call | tf_op jit(solution)/shard_map/attend/pallas_call | solution.py:468
  66.8 37.6 %feed.1 = (bf16[560,768]{1,0:T(8,128)(2,1)}, bf16[560,768]{1,0:T(8,128)(2,1)}, bf16[768,1536]{1,0:T(8,128)(2,1)}, bf16[768,1536]{1,0:T(8,128)(2,1)}, bf16[1536,7...) custom-call(bf16[1120,384]{1,0:T(8,128)(2,1)} %get-tuple-element.72.context_ref, ...), custom_call_target="tpu_custom_call" | custom-call | tf_op jit(solution)/shard_map/feed/pallas_call | solution.py:1861
  104.4 130.4 %finish.1 = (bf16[4608,768]{1,0:T(8,128)(2,1)}, bf16[1120,768]{1,0:T(8,128)(2,1)}, f32[1120,384]{1,0:T(8,128)}, f32[16,768]{1,0:T(8,128)}, f32[64,256]{1,0:T(8,128)}, /*index=5*/bf16[6,1120,1152]{2,1,0:T(8,128)(2,1)}) custom-call(bf16[6,1120,1152]{2,1,0:T(8,128)(2,1)} %get-tuple-element.70.exp_ref, f32[1120,384]{1,0:T(8,128)} %get-tuple-element.71.inverse_ref, ...), custom_call_target="tpu_custom_call" | custom-call | tf_op jit(solution)/shard_map/finish/pallas_call | solution.py:1375
  234.8 12.7 %unpack.1 = (bf16[1089,768]{1,0:T(8,128)(2,1)}, f32[1089,1,384]{2,1,0:T(1,128)}, f32[3,768,384]{2,1,0:T(8,128)}, f32[384,768]{1,0:T(8,128)}, f32[768,1536]{1,0:T...) custom-call(bf16[4608,768]{1,0:T(8,128)(2,1)} %get-tuple-element.89., ...), custom_call_target="tpu_custom_call" | custom-call | tf_op jit(solution)/shard_map/unpack/pallas_call | solution.py:1593
